TPU v7x, 512 devices: a whole 4x4x16 slice. The times are simulated.
512 devices in a mesh: cls: 8 (over x, core), pix: 32 (over z_lo, y), rep: 2 (over z_hi).
Axes of the slice: x: 4, y: 4, z: 16 (z_hi: 2, z_lo: 8; z = z_hi * 8 + z_lo), core: 2. Of those that a mesh axis runs over, the one named last changes fastest.
Arguments:
- particles: float32 [1024, 128, 2, 256], P(('cls', 'rep'), 'pix'), may hold values from -24 to 24
- references: float32 [200, 128, 2, 256], P('cls', 'pix'), may hold values from -10 to 10
- ctf_table: float32 [16, 128], P(None, 'pix'), may hold values from -1 to 1
- defocus_ids: int32 [1024], P(('cls', 'rep')), may hold values from 0 to 15, as said below
- rotation_ids: int32 [36], replicated, may hold values from 0 to 359, as said below
Outputs:
- new_references: float32 [200, 128, 2, 256], P('cls', 'pix')
Inputs may be any that keep to these rules, and one draw needn't show every extreme that they name: `defocus_ids`: the id of particle i is i * 16 // 1024 or one more, at most 15; the first particle's id is 0. `rotation_ids`: rotation a lies in [a * 10, (a + 1) * 10); the first is 0 and the last is 359.
All inputs are finite; a program needn't handle non-finite values.
Results may differ from a plain program's by a relative error of at most 0.0035.
Values may be sent and summed in bfloat16 or wider, within the bound.
A program may use at most 64 MiB of HBM per device.

v0:
```python
import math

import jax
import jax.numpy as jnp
from jax import lax
from jax.sharding import PartitionSpec as P

TURN_STEPS = 360
DEFOCI = 16


EPSILON = 1e-06
SHARPNESS = 30.0
PRIOR_WEIGHT = 1.0


def dft_matrix_of(size):
    positions = jnp.arange(size, dtype=jnp.int32)
    turn_count = positions[:, None] * positions[None, :] % size
    radians = turn_count.astype(jnp.float32) * (2.0 * math.pi / size)
    cosine = jnp.cos(radians) / math.sqrt(size)
    sine_part = jnp.sin(radians) / math.sqrt(size)
    top_half = jnp.concatenate([cosine, -sine_part], axis=1)
    bottom_half = jnp.concatenate([sine_part, cosine], axis=1)
    return jnp.concatenate([top_half, bottom_half], axis=0)


def rotation_phases(rotation_ids, size):
    positions = jnp.arange(size, dtype=jnp.int32)
    signed = jnp.where(positions < size // 2, positions, positions - size)
    turn_count = rotation_ids[:, None] * signed[None, :] % TURN_STEPS
    radians = turn_count.astype(jnp.float32) * (2.0 * math.pi / TURN_STEPS)
    return (jnp.cos(radians), jnp.sin(radians))


def angle_block():
    for attempt in (4, 3, 2, 1):
        return attempt
    return 1


def turned_rows(weighted, cosine, sine_part, first_angle, block_span):
    part_count = weighted.shape[0]
    row_width = weighted.shape[1] * weighted.shape[2] * weighted.shape[3]
    cos_rows = lax.dynamic_slice_in_dim(cosine, first_angle, block_span, 0)[:, None, None, :]
    sin_rows = lax.dynamic_slice_in_dim(sine_part, first_angle, block_span, 0)[:, None, None, :]
    real_part = weighted[None, :, :, 0, :]
    imag_part = weighted[None, :, :, 1, :]
    turned_re = real_part * cos_rows - imag_part * sin_rows
    turned_im = real_part * sin_rows + imag_part * cos_rows
    stacked = jnp.stack([turned_re, turned_im], axis=3).astype(jnp.bfloat16)
    return stacked.reshape(block_span * part_count, row_width)


def correlate_all(weighted, cosine, sine_part, spectra_piece):
    angles = cosine.shape[0]
    block_span = angle_block()
    part_count = weighted.shape[0]
    piece_classes = spectra_piece.shape[0]

    def correlate_angle_step(carried, first_angle):
        rows_now = turned_rows(weighted, cosine, sine_part, first_angle, block_span)
        product = lax.dot_general(
            rows_now, spectra_piece, (((1,), (1,)), ((), ())), preferred_element_type=jnp.float32
        )
        return (carried, product.reshape(block_span, part_count, piece_classes))

    firsts = jnp.arange(0, angles, block_span, dtype=jnp.int32)
    stacked = lax.scan(correlate_angle_step, jnp.zeros((), jnp.int32), firsts)[1]
    return stacked.reshape(angles, part_count, piece_classes)


def defocus_norms(ctf_table, spectra_piece, cycles_here):
    piece_classes = spectra_piece.shape[0]
    squared = jnp.square(spectra_piece.astype(jnp.float32)).reshape(piece_classes, cycles_here, -1)
    cycle_power = jnp.sum(squared, axis=2)
    return jnp.dot(ctf_table * ctf_table, cycle_power.T, precision=lax.Precision.HIGHEST)


def responsibilities(products, part_norm, ref_norm, defocus_pick):
    picked_norm = jnp.dot(defocus_pick, ref_norm, precision=lax.Precision.HIGHEST)
    scaling = (
        lax.rsqrt(part_norm + EPSILON)[None, :, None] * lax.rsqrt(picked_norm + EPSILON)[None, :, :]
    )
    scores = SHARPNESS * products * scaling
    raised = jnp.exp(scores)
    return (raised / jnp.sum(raised, axis=(0, 2), keepdims=True)).astype(jnp.bfloat16)


def class_sums(weighted, cosine, sine_part, weights, class_count):
    angles = cosine.shape[0]
    block_span = angle_block()
    part_count = weighted.shape[0]
    row_width = weighted.shape[1] * weighted.shape[2] * weighted.shape[3]

    def class_angle_step(running, first_angle):
        rows_now = turned_rows(weighted, cosine, sine_part, first_angle, block_span)
        picked = lax.dynamic_slice_in_dim(weights, first_angle, block_span, 0).reshape(
            block_span * part_count, class_count
        )
        update = lax.dot_general(
            picked, rows_now, (((0,), (0,)), ((), ())), preferred_element_type=jnp.float32
        )
        return (running + update, None)

    firsts = jnp.arange(0, angles, block_span, dtype=jnp.int32)
    return lax.scan(class_angle_step, jnp.zeros((class_count, row_width), jnp.float32), firsts)[0]


def per_device(particles, references, ctf_table, defocus_ids, rotation_ids):
    highest = lax.Precision.HIGHEST
    part_count = particles.shape[0]
    cycles_here = particles.shape[1]
    samples = particles.shape[3]
    classes_here = references.shape[0]
    row_width = cycles_here * 2 * samples
    dft_matrix = dft_matrix_of(samples)
    spectra = jnp.dot(
        particles.reshape(part_count * cycles_here, 2 * samples), dft_matrix, precision=highest
    )
    spectra = spectra.reshape(part_count, cycles_here, 2, samples)
    defocus_pick = (defocus_ids[:, None] == jnp.arange(DEFOCI, dtype=jnp.int32)[None, :]).astype(
        jnp.float32
    )
    ctf_rows = jnp.dot(defocus_pick, ctf_table, precision=highest)
    weighted = ctf_rows[:, :, None, None] * spectra
    cosine, sine_part = rotation_phases(rotation_ids, samples)
    part_norm = jnp.sum(particles * particles, axis=(1, 2, 3))
    own_spectra = jnp.dot(
        references.reshape(classes_here * cycles_here, 2 * samples), dft_matrix, precision=highest
    )
    own_spectra = own_spectra.astype(jnp.bfloat16).reshape(classes_here, row_width)
    every_spectra = lax.all_gather(own_spectra, "cls", axis=0, tiled=True)
    products = correlate_all(weighted, cosine, sine_part, every_spectra)
    ref_norm = defocus_norms(ctf_table, every_spectra, cycles_here)
    products, part_norm, ref_norm = lax.psum((products, part_norm, ref_norm), "pix")
    weights = responsibilities(products, part_norm, ref_norm, defocus_pick)
    presence = jnp.sum(weights.astype(jnp.float32), axis=0)
    density = lax.psum(jnp.dot(presence.T, ctf_rows * ctf_rows, precision=highest), ("cls", "rep"))
    owned = lax.psum_scatter(
        class_sums(weighted, cosine, sine_part, weights, classes_here * lax.axis_size("cls")),
        "cls",
        scatter_dimension=0,
        tiled=True,
    )
    owned = lax.psum(owned, "rep")
    owned_density = lax.dynamic_slice_in_dim(
        density, lax.axis_index("cls") * classes_here, classes_here, 0
    )
    new_spectra = owned.reshape(classes_here * cycles_here, 2 * samples) / (
        owned_density.reshape(classes_here * cycles_here, 1) + PRIOR_WEIGHT
    )
    new_rows = jnp.dot(new_spectra, dft_matrix.T, precision=highest)
    return new_rows.reshape(classes_here, cycles_here, 2, samples)


def solution(mesh):
    in_specs = (
        P(("cls", "rep"), "pix", None, None),
        P("cls", "pix", None, None),
        P(None, "pix"),
        P(("cls", "rep")),
        P(),
    )
    out_specs = P("cls", "pix", None, None)
    return jax.shard_map(
        per_device, mesh=mesh, in_specs=in_specs, out_specs=out_specs, check_vma=False
    )
```

profile of v0, /device:TPU:1, one launch (start us, length us, event | category | flops | bytes accessed | tf_op | source)
XLA Modules:
  0.0 878.1 jit_solution(17126335464374318957)
XLA Ops:
  9.8 1.8 convolution_bitcast_fusion.1
  14.8 20.6 %all-gather = bf16[8,25,2048]{2,1,0:T(8,128)(2,1)S(1)} all-gather(bf16[1,25,2048]{2,1,0:T(8,128)(2,1)S(1)} %reshape.130), channel_id=1, replica_groups=mesh['cls'=8,'pix'=32,'rep'=2] {'cls'}, dimensions={0}, use_global_device_ids=true | all-gather | bytes 921600 | tf_op jit(solution)/shard_map/all_gather | solution.py:133
  36.0 92.4 %while.21 = (s32[]{:T(128)}, f32[9,4,64,200]{3,2,1,0:T(8,128)}, f32[64,4,2,256]{3,1,0,2:T(4,128)}, s32[9]{0:T(128)S(1)}, f32[36,256]{1,0:T(8,128)S(1)}, /*index=...) while((s32[]{:T(128)}, f32[9,4,64,200]{3,2,1,0:T(8,128)}, ...), condition=%wide.region_1.2_spmd, body=%wide.region_0.1_spmd.sunk | while | flops 213909504 | bytes 8970903 | solution.py:69
  39.6 2.2 subtract_convert_fusion.4
  41.8 2.4 pad_maximum_fusion.4
  49.8 2.2 subtract_convert_fusion.4
  52.0 2.4 pad_maximum_fusion.4
  60.1 2.2 subtract_convert_fusion.4
  62.3 2.4 pad_maximum_fusion.4
  65.6 1.2 fusion.50
  70.4 2.2 subtract_convert_fusion.4
  72.6 2.4 pad_maximum_fusion.4
  80.6 2.2 subtract_convert_fusion.4
  82.9 2.4 pad_maximum_fusion.4
  86.1 1.2 fusion.50
  90.9 2.2 subtract_convert_fusion.4
  93.1 2.4 pad_maximum_fusion.4
  101.2 2.2 subtract_convert_fusion.4
  103.4 2.4 pad_maximum_fusion.4
  111.4 2.2 subtract_convert_fusion.4
  113.6 2.4 pad_maximum_fusion.4
  121.7 2.2 subtract_convert_fusion.4
  123.9 2.4 pad_maximum_fusion.4
  127.2 1.2 fusion.50
  129.2 2.3 reshape.129
  131.5 1.7 reduce_sum.37
  133.2 1.3 dynamic-slice.4
  136.0 207.1 %all-reduce.2 = (f32[16,200]{1,0:T(8,128)S(1)}, f32[64]{0:T(128)S(1)}) all-reduce(f32[16,200]{1,0:T(8,128)S(1)} %fusion.29, f32[64]{0:T(128)S(1)} %multiply_reduce_fusion), channel_id=1, replica_groups=mesh['cls'=8,'pix'=32,'rep'=2] {'pix'}, use_global_device_ids=true, to_apply=%region_6.7 | all-reduce | flops 3264 | bytes 26112 | tf_op jit(solution)/shard_map/psum | solution.py:136
  344.5 220.8 %all-reduce.6.cloned.1.call-done = f32[36,64,200]{2,1,0:T(8,128)} async-done(((f32[36,64,200]{2,1,0:T(8,128)}), f32[36,64,200]{2,1,0:T(8,128)}) %all-reduce.6.cloned.1.call-update) | async-done | bytes 1843216 | tf_op jit(solution)/shard_map/psum | solution.py:136
  565.3 2.3 fusion.3
  567.7 1.6 convert_reduce_fusion
  569.3 119.6 %while.22 = (s32[]{:T(128)}, f32[200,2048]{1,0:T(8,128)}, s32[9]{0:T(128)S(1)}, bf16[36,64,200]{2,1,0:T(8,128)(2,1)}, f32[64,4,2,256]{3,2,1,0:T(2,128)S(1)}, /*i...) while((s32[]{:T(128)}, f32[200,2048]{1,0:T(8,128)}, ...), condition=%wide.region_9.10_spmd.clone, body=%wide.region_8.9_spmd.clone.sunk | while | flops 214728704 | bytes 12521637 | solution.py:107
  573.3 2.2 subtract_convert_fusion.5
  575.5 2.4 pad_maximum_fusion.5
  579.7 1.6 convolution_add_fusion.3
  585.3 2.2 subtract_convert_fusion.5
  587.5 2.4 pad_maximum_fusion.5
  591.7 3.0 convolution_add_fusion.3
  598.7 2.2 subtract_convert_fusion.5
  600.9 2.4 pad_maximum_fusion.5
  605.1 3.0 convolution_add_fusion.3
  612.2 2.2 subtract_convert_fusion.5
  614.4 2.4 pad_maximum_fusion.5
  618.6 3.0 convolution_add_fusion.3
  625.6 2.2 subtract_convert_fusion.5
  627.8 2.4 pad_maximum_fusion.5
  632.0 3.0 convolution_add_fusion.3
  639.1 2.2 subtract_convert_fusion.5
  641.3 2.4 pad_maximum_fusion.5
  645.5 3.0 convolution_add_fusion.3
  652.5 2.2 subtract_convert_fusion.5
  654.7 2.4 pad_maximum_fusion.5
  658.9 3.0 convolution_add_fusion.3
  665.9 2.2 subtract_convert_fusion.5
  668.2 2.4 pad_maximum_fusion.5
  672.4 3.0 convolution_add_fusion.3
  679.4 2.2 subtract_convert_fusion.5
  681.6 2.4 pad_maximum_fusion.5
  685.8 3.0 convolution_add_fusion.3
  688.8 40.6 %fusion = f32[32,2048]{1,0:T(8,128)S(1)} fusion(f32[200,2048]{1,0:T(8,128)} %get-tuple-element.80), kind=kCustom, calls=%all-reduce-scatter | all-reduce-scatter fusion | flops 524289 | bytes 1902592
  729.4 2.8 collective-permute-start
  732.3 2.6 collective-permute-start.1
  735.0 69.9 %psum.39 = f32[200,4]{0,1:T(4,128)S(1)} all-reduce(f32[200,4]{0,1:T(4,128)S(1)} %fusion.27), channel_id=1, replica_groups=mesh['cls'=8,'pix'=32,'rep'=2] {'cls','rep'}, use_global_device_ids=true, to_apply=%region_13.14 | all-reduce | flops 800 | bytes 6400 | tf_op jit(solution)/shard_map/psum | solution.py:139
  806.6 61.5 %all-reduce.8.cloned.1.call-done = f32[25,2048]{1,0:T(8,128)} async-done(((f32[25,2048]{1,0:T(8,128)}), f32[25,2048]{1,0:T(8,128)}) %all-reduce.8.cloned.1.call-update) | async-done | bytes 204816 | tf_op jit(solution)/shard_map/psum | solution.py:146
  (174 shorter events, 77.4 us)
Async XLA Ops:
  6.5 558.8 %all-reduce.6.cloned.1.call-start = ((), (), s32[]{:S(2)}) async-start(), calls=%async_computation | async-start | bytes 4718592 | tf_op jit(solution)/shard_map/psum | solution.py:136
  7.6 6.3 copy-start.3
  7.6 6.3 copy-start.5
  8.6 5.3 copy-start.7
  9.8 2.4 copy-start.11
  9.8 2.4 copy-start.13
  11.6 2.2 copy-start.9
  14.7 21.0 %copy-start.12 = (s32[36]{0:T(128)S(1)}, s32[36]{0:T(128)}, u32[]{:S(2)}) copy-start(s32[36]{0:T(128)} %param.13) | copy-start | bytes 436
  128.3 0.6 copy-start.10
  128.4 0.6 copy-start.15
  128.4 739.7 %all-reduce.8.cloned.1.call-start = ((), (), s32[]{:S(2)}) async-start(), calls=%async_computation.1 | async-start | bytes 524288 | tf_op jit(solution)/shard_map/psum | solution.py:146
  129.2 6.0 copy-start.2
  129.2 214.0 %copy-start.4 = (f32[256,256]{1,0:T(8,128)S(1)}, f32[256,256]{1,0:T(8,128)}, u32[]{:S(2)}) copy-start(f32[256,256]{1,0:T(8,128)} %copy-done.3) | copy-start | bytes 786436
  129.2 214.0 %copy-start.6 = (f32[256,256]{1,0:T(8,128)S(1)}, f32[256,256]{1,0:T(8,128)}, u32[]{:S(2)}) copy-start(f32[256,256]{1,0:T(8,128)} %copy-done.5) | copy-start | bytes 786436
  129.2 213.9 %copy-start.8 = (f32[256,256]{1,0:T(8,128)S(1)}, f32[256,256]{1,0:T(8,128)}, u32[]{:S(2)}) copy-start(f32[256,256]{1,0:T(8,128)} %copy-done.7) | copy-start | bytes 786436
  131.5 212.8 %copy-start.14 = (s32[64]{0:T(128)S(1)}, s32[64]{0:T(128)}, u32[]{:S(2)}) copy-start(s32[64]{0:T(128)} %param.12) | copy-start | bytes 772
  565.3 2.4 copy-start
  567.7 1.6 copy-start.16
  729.4 75.7 %collective-permute-start = (f32[32,2048]{1,0:T(8,128)S(1)}, f32[32,2048]{1,0:T(8,128)S(1)}, u32[]{:S(2)}, u32[]{:S(2)}) collective-permute-start(f32[32,2048]{1,0:T(8,128)S(1)} %fusion), channel_id=1, source_target_pairs={{0,64},{64,128},{128,192},{192,256},{256,320},{320,384},{384,448},... | collective-permute-start | bytes 786440
  732.3 72.9 %collective-permute-start.1 = (f32[17,2048]{1,0:T(8,128)S(1)}, f32[17,2048]{1,0:T(8,128)S(1)}, u32[]{:S(2)}, u32[]{:S(2)}) collective-permute-start(f32[17,2048]{1,0:T(8,128)S(1)} %slice.14), channel_id=1, source_target_pairs={{0,128},{64,192},{128,256},{192,320},{256,384},{320,448},{1,129},{... | collective-permute-start | bytes 417800
  805.1 64.1 %copy-start.1 = (f32[512,512]{1,0:T(8,128)S(1)}, f32[512,512]{1,0:T(8,128)}, u32[]{:S(2)}) copy-start(f32[512,512]{1,0:T(8,128)} %maximum_maximum_fusion) | copy-start | bytes 3145732
Sparse Core Ops, SparseCore 0:
  128.5 436.7 all-reduce.5
  806.5 61.5 all-reduce.7
where the time goes:
time: 880 us; the launch traced here: 878 us
  blocking collectives  338 us (38%)
  waiting for transfers between devices  282 us (32%)
  other arithmetic  94.8 us (11%)
  local copies, waits for them, and re-layouts  65.4 us (7%)
  matrix products  41.1 us (5%)
  loops' own time  36.2 us (4%)
  between operations  14.4 us (2%)
    psum x1, waiting for transfers between devices, per_device(): lax.psum((products, part_norm, ref_norm), 'pix')  221 us
    psum x1, blocking collectives, per_device(): lax.psum((products, part_norm, ref_norm), 'pix')  207 us
    psum x1, blocking collectives, per_device(): lax.psum(jnp.dot(presence.T, ctf_rows * ctf_rows, precision=highest), ('c...  69.9 us
    psum x1, waiting for transfers between devices, per_device(): owned = lax.psum(owned, 'rep')  61.5 us
    another operation x18, other arithmetic, turned_rows(): stacked = jnp.stack([turned_re, turned_im], axis=3).astype(jnp.bfloat16)  43.8 us
    unnamed x1, blocking collectives  40.6 us
    another operation x18, other arithmetic  39.8 us
    dot_general x9, matrix products, class_angle_step(): lax.dot_general(picked, rows_now, (((0,), (0,)), ((), ())), preferred_ele...  26 us
  transfers between devices with their start and end apart: 4, of which 2 were waited for; matrix products, arithmetic and copies ran while one was open for 1% of the time, Pallas kernels for 0%

commit v1 on v0

v1 whole, which is shorter than its diff:
```python
import math

import jax
import jax.numpy as jnp
import numpy as np
from jax import lax
from jax.experimental import pallas as pl
from jax.experimental.pallas import tpu as pltpu
from jax.sharding import PartitionSpec as P

TURN_STEPS = 360
DEFOCI = 16
EPSILON = 1e-06
SHARPNESS = 30.0
PRIOR_WEIGHT = 1.0

F32 = jnp.float32
BF16 = jnp.bfloat16
MESH = pl.DeviceIdType.MESH

SAMPLES = 256
ANGLES = 36
TURN_ROWS = 40
PAIR_ROWS = 2 * TURN_ROWS
PARTICLES_HERE = 64
CYCLES_HERE = 4
CLASSES_HERE = 25
BLOCK = 32
NX, NY, NZ = 4, 4, 8
ALL_CLASSES = 2 * NX * BLOCK
SIDE = 128
ROW_WIDTH = SIDE + CYCLES_HERE * 2 * SAMPLES
GROUPS = 4
Y_ROWS = 2 * PAIR_ROWS
GROUP_ROWS = NY * Y_ROWS
ALL_ROWS = GROUPS * GROUP_ROWS

NN = (((1,), (0,)), ((), ()))
NT = (((1,), (1,)), ((), ()))
TN = (((0,), (0,)), ((), ()))


def dft_matrix():
    positions = np.arange(SAMPLES)
    radians = (positions[:, None] * positions[None, :] % SAMPLES) * (2.0 * math.pi / SAMPLES)
    cosine = np.cos(radians) / math.sqrt(SAMPLES)
    sine = np.sin(radians) / math.sqrt(SAMPLES)
    return np.block([[cosine, -sine], [sine, cosine]]).astype(np.float32)


def walsh_matrix():
    matrix = np.ones((1, 1), np.float32)
    while matrix.shape[0] < ALL_CLASSES:
        matrix = np.block([[matrix, matrix], [matrix, -matrix]])
    return matrix


def split(values):
    high = values.astype(BF16)
    return high, (values - high.astype(F32)).astype(BF16)


def walsh(values, walsh_ref):
    high, low = split(values)
    return lax.dot_general(high, walsh_ref[...], NN, preferred_element_type=F32) + lax.dot_general(
        low, walsh_ref[...], NN, preferred_element_type=F32
    )


def dft(values, high_ref, low_ref):
    high, low = split(values)
    return (
        lax.dot_general(high, high_ref[...], NN, preferred_element_type=F32)
        + lax.dot_general(low, high_ref[...], NN, preferred_element_type=F32)
        + lax.dot_general(high, low_ref[...], NN, preferred_element_type=F32)
    )


def body(
    x_hbm, r_hbm, dft_hbm, walsh_hbm, ctf_hbm, ids_hbm, turns_hbm, out_ref,
    x_ref, r_ref, dft_ref, walsh_f, ctf_in, ids_ref, turns_ref,
    high_ref, low_ref, walsh_ref, ctf_ref, phase_ref,
    padded, x_rows, r_rows, spectra, weighted, power_rows, norm_rows, turned,
    partial_f, partial, far_in, near_in, near_out, z_out, z_in, z_sum, pair_out, pair_in, weights,
    sums, core_out, core_in, xfar_out, xfar_in, xnear_out, xnear_in, rep_out, rep_via, rep_in,
    in_sem, rx_s, rx_r, rf_s, rf_r, rc_s, rc_r,
    fs, fr, ns, nr, zs, zr, zps, zpr, wps, wpr, wzs, wzr, wys, wyr, wfs, wfr,
    cs, cr, xfs, xfr, xns, xnr, p1s, p1r, p2s, p2r,
):
    loads = [
        pltpu.make_async_copy(src, dst, in_sem.at[n])
        for n, (src, dst) in enumerate(
            [
                (r_hbm, r_ref), (dft_hbm, dft_ref), (x_hbm, x_ref), (ids_hbm, ids_ref),
                (turns_hbm, turns_ref), (ctf_hbm, ctf_in), (walsh_hbm, walsh_f),
            ]
        )
    ]
    for load in loads:
        load.start()
    cls = lax.axis_index("cls")
    pix = lax.axis_index("pix")
    rep = lax.axis_index("rep")
    x, core = cls // 2, cls % 2
    z, y = pix // NY, pix % NY
    other = 1 - core
    sibling = {"cls": x * 2 + other}

    def x_peer(d):
        return {"cls": (x + d) % NX * 2 + core}

    def y_peer(d):
        return {"pix": z * NY + (y + d) % NY}

    q, zh = z % 4, z // 4

    def q_peer(q_to):
        return {"pix": (zh * 4 + q_to) * NY + y}

    z_pair = {"pix": (z + 4) % NZ * NY + y}

    far_z = (z + 4) % NZ
    up = (z + 4) // NZ
    via = (
        {"pix": far_z * NY + y, "rep": (rep + up) % 2},
        {"pix": far_z * NY + y, "rep": (rep + 1 - up) % 2},
    )
    partners = (
        [sibling, {"pix": far_z * NY + y, "rep": 1 - rep}]
        + [x_peer(d) for d in (1, 3)]
        + [y_peer(d) for d in (1, 3)]
        + [q_peer((q + d) % 4) for d in range(1, 4)]
        + [z_pair]
    )

    def remote(src, dst, send, recv, device):
        return pltpu.make_async_remote_copy(
            src_ref=src, dst_ref=dst, send_sem=send, recv_sem=recv,
            device_id=device, device_id_type=MESH,
        )

    sent = []

    def start_copy(*args):
        remote(*args).start()

    def send(*args):
        copy = remote(*args)
        copy.start()
        sent.append(copy)

    barrier = pltpu.get_barrier_semaphore()
    for partner in partners:
        pl.semaphore_signal(barrier, inc=1, device_id=partner, device_id_type=MESH)

    loads[0].wait()
    loads[1].wait()
    high, low = split(dft_ref[...])
    high_ref[...] = high
    low_ref[...] = low
    padded[...] = jnp.zeros_like(padded)
    padded[0 : CLASSES_HERE * 16, :] = r_ref[...]
    for r in range(CYCLES_HERE):
        for p in range(2):
            for h in range(2):
                r_rows[r * BLOCK : (r + 1) * BLOCK, p * 256 + h * 128 : p * 256 + h * 128 + 128] = padded[
                    pl.ds(r * 4 + h * 2 + p, BLOCK, stride=16), :
                ]
    own = dft(r_rows[...], high_ref, low_ref).astype(BF16)
    own_rows = pl.ds(pl.multiple_of(cls * BLOCK, BLOCK), BLOCK)
    wide = own.astype(F32)
    power = jnp.sum(wide * wide, axis=1, keepdims=True)
    power_high, power_low = split(power)
    side_lane = lax.broadcasted_iota(jnp.int32, (BLOCK, SIDE), 1)
    side = jnp.zeros((BLOCK, SIDE), F32)
    for r in range(CYCLES_HERE):
        rows = slice(r * BLOCK, (r + 1) * BLOCK)
        spectra[own_rows, SIDE + r * 512 : SIDE + (r + 1) * 512] = own[rows, :]
        side = jnp.where(side_lane == r, power_high.astype(F32)[rows, :], side)
        side = jnp.where(side_lane == CYCLES_HERE + r, power_low.astype(F32)[rows, :], side)
    spectra[own_rows, 0:SIDE] = side.astype(BF16)

    pl.semaphore_wait(barrier, len(partners))
    steps = (1, 3)
    for way in range(2):
        send(
            spectra.at[own_rows, :], spectra.at[own_rows, :],
            rx_s.at[way], rx_r.at[way], x_peer(steps[way]),
        )
    send(spectra.at[own_rows, :], spectra.at[own_rows, :], rc_s.at[0], rc_r.at[0], sibling)

    def class_rows(x_of, core_of):
        return pl.ds(pl.multiple_of((x_of * 2 + core_of) * BLOCK, BLOCK), BLOCK)

    def half_rows(x_of, core_of, half):
        start = (x_of * 2 + core_of) * BLOCK + half * (BLOCK // 2)
        return pl.ds(pl.multiple_of(start, BLOCK // 2), BLOCK // 2)

    for load in loads[2:]:
        load.wait()
    walsh_ref[...] = walsh_f[...].astype(BF16)
    select = (
        lax.broadcasted_iota(jnp.int32, (CYCLES_HERE, 128), 1)
        - lax.broadcasted_iota(jnp.int32, (CYCLES_HERE, 128), 0)
    )
    select = ((select == 0) | (select == CYCLES_HERE)).astype(F32)
    ctf_ref[...] = lax.dot_general(
        ctf_in[...], select, TN, precision=lax.Precision.HIGHEST, preferred_element_type=F32
    )
    shape = (TURN_ROWS, ANGLES)
    on_row = lax.broadcasted_iota(jnp.int32, shape, 0) == lax.broadcasted_iota(jnp.int32, shape, 1)
    turns = jnp.sum(
        jnp.where(on_row, jnp.broadcast_to(turns_ref[...].astype(F32), shape), 0.0),
        axis=1, keepdims=True,
    )
    place = lax.broadcasted_iota(jnp.int32, (TURN_ROWS, SAMPLES), 1)
    signed = jnp.where(place < SAMPLES // 2, place, place - SAMPLES).astype(F32)
    count = turns * signed
    count = count - TURN_STEPS * jnp.floor(count * (1.0 / TURN_STEPS))
    count = jnp.where(count < 0, count + TURN_STEPS, count)
    count = jnp.where(count >= TURN_STEPS, count - TURN_STEPS, count)
    radians = count * (2.0 * math.pi / TURN_STEPS)
    phase_ref[0:TURN_ROWS, :] = jnp.cos(radians)
    phase_ref[TURN_ROWS : 2 * TURN_ROWS, :] = jnp.sin(radians)

    for r in range(CYCLES_HERE):
        for p in range(2):
            for h in range(2):
                x_rows[r * 64 : (r + 1) * 64, p * 256 + h * 128 : p * 256 + h * 128 + 128] = x_ref[
                    pl.ds(r * 4 + h * 2 + p, PARTICLES_HERE, stride=16), :
                ]
    part_square = jnp.zeros((PARTICLES_HERE, 128), F32)
    for r in range(CYCLES_HERE):
        for h in range(4):
            piece = x_rows[r * 64 : (r + 1) * 64, h * 128 : (h + 1) * 128]
            part_square += piece * piece
    part_norm = jnp.sum(part_square, axis=1, keepdims=True)
    picks = (
        lax.broadcasted_iota(jnp.int32, (DEFOCI, PARTICLES_HERE), 0) == ids_ref[...]
    ).astype(F32)
    ctf_rows = lax.dot_general(
        picks, ctf_ref[...], TN, precision=lax.Precision.HIGHEST, preferred_element_type=F32
    )
    particle_spectra = dft(x_rows[...], high_ref, low_ref)
    for r in range(CYCLES_HERE):
        weighted[:, r * 512 : (r + 1) * 512] = (
            ctf_rows[:, r : r + 1] * particle_spectra[r * 64 : (r + 1) * 64, :]
        )
    squared = ctf_rows * ctf_rows
    square_high = squared.astype(BF16).astype(F32)
    lane = lax.broadcasted_iota(jnp.int32, squared.shape, 1)
    power_rows[...] = jnp.where(lane < CYCLES_HERE, square_high, squared - square_high)

    for way in range(2):
        x_of = (x + NX - steps[way]) % NX
        rows = spectra.at[class_rows(x_of, core), :]
        remote(rows, rows, rx_s.at[way], rx_r.at[way], x_peer(steps[way])).wait_recv()
        half = spectra.at[half_rows(x_of, core, way), :]
        send(half, half, rf_s.at[way], rf_r.at[way], x_peer(steps[way]))
        send(rows, rows, rc_s.at[way + 1], rc_r.at[way + 1], sibling)

    cosine = phase_ref[0:TURN_ROWS, :]
    sine = phase_ref[TURN_ROWS : 2 * TURN_ROWS, :]

    def turn_pair(pair, carry):
        rows = pl.ds(pl.multiple_of(pair * PAIR_ROWS, 16), PAIR_ROWS)
        for r in range(CYCLES_HERE):
            real, imag = [], []
            for e in range(2):
                w_re = weighted[pl.ds(pair * 2 + e, 1), r * 512 : r * 512 + 256]
                w_im = weighted[pl.ds(pair * 2 + e, 1), r * 512 + 256 : r * 512 + 512]
                real.append(w_re * cosine - w_im * sine)
                imag.append(w_re * sine + w_im * cosine)
            start = SIDE + r * 512
            turned[rows, start : start + 256] = jnp.concatenate(real, axis=0).astype(BF16)
            turned[rows, start + 256 : start + 512] = jnp.concatenate(imag, axis=0).astype(BF16)
        tail = [
            jnp.broadcast_to(power_rows[pl.ds(pair * 2 + e, 1), :], (TURN_ROWS, 128)) for e in range(2)
        ]
        turned[rows, 0:SIDE] = jnp.concatenate(tail, axis=0).astype(BF16)
        return carry

    lax.fori_loop(0, PARTICLES_HERE // 4, turn_pair, 0)
    x_far = (x + 2) % NX
    for way in range(2):
        half = spectra.at[half_rows(x_far, core, way), :]
        remote(half, half, rf_s.at[way], rf_r.at[way], x_peer(steps[way])).wait_recv()
    rows = spectra.at[class_rows(x_far, core), :]
    send(rows, rows, rc_s.at[3], rc_r.at[3], sibling)
    lax.fori_loop(PARTICLES_HERE // 4, PARTICLES_HERE // 2, turn_pair, 0)

    for n, x_of in enumerate((x, (x + 3) % NX, (x + 1) % NX, x_far)):
        rows = spectra.at[class_rows(x_of, other), :]
        remote(rows, rows, rc_s.at[n], rc_r.at[n], sibling).wait_recv()

    ctf_high, ctf_low = split(ctf_ref[...] * ctf_ref[...])
    ref_norm = lax.dot_general(
        ctf_high, spectra[:, 0:SIDE], NT, preferred_element_type=F32
    ) + lax.dot_general(ctf_low, spectra[:, 0:SIDE], NT, preferred_element_type=F32)
    picked = lax.dot_general(
        picks, ref_norm, TN, precision=lax.Precision.HIGHEST, preferred_element_type=F32
    )
    picked_high = picked.astype(BF16).astype(F32)
    wide_norm = jnp.broadcast_to(part_norm, (PARTICLES_HERE, ALL_CLASSES))
    wide_high = wide_norm.astype(BF16).astype(F32)
    norm_rows[0] = picked_high
    norm_rows[1] = picked - picked_high
    norm_rows[2] = wide_high
    norm_rows[3] = wide_norm - wide_high
    sub = lax.broadcasted_iota(jnp.int32, (8, ALL_CLASSES), 0)

    def z_group(step):
        return (q + 1 + step) % GROUPS

    def y_rows_of(group, y_to):
        return pl.ds(pl.multiple_of(group * GROUP_ROWS + y_to * Y_ROWS, Y_ROWS), Y_ROWS)

    def y_half_of(group, y_to, half):
        start = group * GROUP_ROWS + y_to * Y_ROWS + half * PAIR_ROWS
        return pl.ds(pl.multiple_of(start, PAIR_ROWS), PAIR_ROWS)

    def correlate(step):
        group = z_group(step)
        rows = pl.ds(pl.multiple_of(group * GROUP_ROWS, GROUP_ROWS), GROUP_ROWS)
        partial_f[...] = walsh(
            lax.dot_general(turned[rows, SIDE:], spectra[:, SIDE:], NT, preferred_element_type=F32), walsh_ref
        )

        def patch(pair, carry):
            pieces = []
            for e in range(2):
                start = pl.multiple_of(pair * PAIR_ROWS + e * TURN_ROWS, 8)
                pieces.append(partial_f[pl.ds(start, 32), :])
                last = partial_f[pl.ds(start + 32, 8), :]
                particle = group * 16 + pair * 2 + e
                for n in range(4):
                    last = jnp.where(sub == 4 + n, norm_rows[n, pl.ds(particle, 1), :], last)
                pieces.append(last)
            start = pl.multiple_of(group * GROUP_ROWS + pair * PAIR_ROWS, 16)
            partial[pl.ds(start, PAIR_ROWS), :] = jnp.concatenate(pieces, axis=0).astype(BF16)
            return carry

        lax.fori_loop(0, NY * 2, patch, 0)
        for way in range(2):
            start_copy(
                partial.at[y_half_of(group, (y + 2) % NY, way), :],
                far_in.at[step, way], fs.at[step, way], fr.at[step, way], y_peer(steps[way]),
            )
        for way in range(2):
            start_copy(
                partial.at[y_half_of(group, (y + steps[way]) % NY, 1 - way), :],
                near_in.at[step, way, 1 - way],
                ns.at[step, way, 1 - way], nr.at[step, way, 1 - way], y_peer(steps[way]),
            )

    odd_row = sub % 2 == 1

    def product_rounded(total):
        pieces = []
        for e in range(2):
            start = e * TURN_ROWS
            pieces.append(total[start : start + 32, :])
            last = total[start + 32 : start + 40, :]
            whole = last + pltpu.roll(last, 7, 0)
            high = whole.astype(BF16).astype(F32)
            low = pltpu.roll(whole - high, 1, 0)
            pieces.append(jnp.where(sub < 4, last, jnp.where(odd_row, low, high)))
        return jnp.concatenate(pieces, axis=0).astype(BF16)

    def relay(step):
        group = z_group(step)
        for way in range(2):
            own = partial.at[y_half_of(group, (y + steps[way]) % NY, way), :]
            remote(
                own, far_in.at[step, way], fs.at[step, way], fr.at[step, way], y_peer(steps[way])
            ).wait_recv()
            near_out[step, way] = product_rounded(
                own[...].astype(F32) + far_in[step, way].astype(F32)
            )
            start_copy(
                near_out.at[step, way], near_in.at[step, way, way],
                ns.at[step, way, way], nr.at[step, way, way], y_peer(steps[way]),
            )

    def reduce_y(step):
        group = z_group(step)
        for half in range(2):
            own = partial.at[y_half_of(group, y, half), :]
            total = own[...].astype(F32)
            for way in range(2):
                remote(
                    own, near_in.at[step, way, half],
                    ns.at[step, way, half], nr.at[step, way, half], y_peer(steps[way]),
                ).wait_recv()
                total += near_in[step, way, half].astype(F32)
            z_out[step, half * PAIR_ROWS : (half + 1) * PAIR_ROWS, :] = product_rounded(total)

        @pl.when(step < GROUPS - 1)
        def _():
            start_copy(
                z_out.at[step], z_in.at[step], zs.at[step], zr.at[step], q_peer(group)
            )

    def product_step(step, carry):
        pl.when(step < GROUPS)(lambda: correlate(step))
        pl.when((step > 0) & (step <= GROUPS))(lambda: relay(step - 1))
        pl.when(step > 1)(lambda: reduce_y(step - 2))
        return carry

    lax.fori_loop(0, GROUPS + 2, product_step, 0)

    total = z_out[GROUPS - 1].astype(F32)
    for n in range(GROUPS - 1):
        remote(z_out.at[n], z_in.at[n], zs.at[n], zr.at[n], z_pair).wait_recv()
        total += z_in[n].astype(F32)
    z_sum[...] = total
    pair_out[...] = product_rounded(
        z_sum[pl.ds(pl.multiple_of((1 - zh) * PAIR_ROWS, 16), PAIR_ROWS), :]
    )
    send(pair_out, pair_in, zps, zpr, z_pair)
    mine = z_sum[pl.ds(pl.multiple_of(zh * PAIR_ROWS, 16), PAIR_ROWS), :]
    sums[...] = jnp.zeros_like(sums)
    remote(pair_out, pair_in, zps, zpr, z_pair).wait_recv()
    mine += pair_in[...].astype(F32)

    shape = (TURN_ROWS, ALL_CLASSES)
    valid = (lax.broadcasted_iota(jnp.int32, shape, 0) < ANGLES) & (
        lax.broadcasted_iota(jnp.int32, shape, 1) % BLOCK < CLASSES_HERE
    )
    products = walsh(mine, walsh_ref) * (1.0 / ALL_CLASSES)
    pieces = []
    for e in range(2):
        rows = mine[e * TURN_ROWS : (e + 1) * TURN_ROWS, :]
        ref_row = rows[36:37, :] + rows[37:38, :]
        part_row = rows[38:39, :] + rows[39:40, :]
        scaling = lax.rsqrt(part_row + EPSILON) * lax.rsqrt(ref_row + EPSILON)
        scores = jnp.where(
            valid, SHARPNESS * products[e * TURN_ROWS : (e + 1) * TURN_ROWS, :] * scaling, 0.0
        )
        raised = jnp.where(valid, jnp.exp(scores), 0.0)
        total = jnp.sum(jnp.sum(raised, axis=0, keepdims=True), axis=1, keepdims=True)
        pieces.append(raised / total)

    own_pair = weights.at[y_half_of(q, y, zh), :]
    own_pair[...] = jnp.concatenate(pieces, axis=0).astype(BF16)
    send(own_pair, own_pair, wps, wpr, z_pair)
    pair = weights.at[y_half_of(q, y, 1 - zh), :]
    remote(pair, pair, wps, wpr, z_pair).wait_recv()
    group_rows = weights.at[y_rows_of(q, y), :]
    for d in (1, 3, 2):
        send(group_rows, group_rows, wzs.at[d], wzr.at[d], q_peer((q + d) % 4))

    def w_group(step):
        return (q + GROUPS - step) % GROUPS

    def spread(step):
        group = w_group(step)
        rows = weights.at[y_rows_of(group, y), :]

        @pl.when(step > 0)
        def _():
            remote(rows, rows, wzs.at[step], wzr.at[step], z_pair).wait_recv()

        for way in range(2):
            start_copy(rows, rows, wys.at[step, way], wyr.at[step, way], y_peer(steps[way]))

    def pass_on(step):
        group = w_group(step)
        for way in range(2):
            y_of = (y + NY - steps[way]) % NY
            rows = weights.at[y_rows_of(group, y_of), :]
            remote(
                rows, rows, wys.at[step, way], wyr.at[step, way], y_peer(steps[way])
            ).wait_recv()
            half = weights.at[y_half_of(group, y_of, way), :]
            start_copy(half, half, wfs.at[step, way], wfr.at[step, way], y_peer(steps[way]))

    def add_group(step):
        group = w_group(step)
        for way in range(2):
            half = weights.at[y_half_of(group, (y + 2) % NY, way), :]
            remote(
                half, half, wfs.at[step, way], wfr.at[step, way], y_peer(steps[way])
            ).wait_recv()
        rows = pl.ds(pl.multiple_of(group * GROUP_ROWS, GROUP_ROWS), GROUP_ROWS)
        picked_weights = weights[rows, :].T
        sums[:, 0:SIDE] += lax.dot_general(
            picked_weights, turned[rows, 0:SIDE], NN, preferred_element_type=F32
        )
        for r in range(CYCLES_HERE):
            lanes = slice(SIDE + r * 512, SIDE + (r + 1) * 512)
            sums[:, lanes] += lax.dot_general(
                picked_weights, turned[rows, lanes], NN, preferred_element_type=F32
            )

    def weight_step(step, carry):
        pl.when(step < GROUPS)(lambda: spread(step))
        pl.when((step > 0) & (step <= GROUPS))(lambda: pass_on(step - 1))
        pl.when(step > 1)(lambda: add_group(step - 2))
        return carry

    lax.fori_loop(0, GROUPS + 2, weight_step, 0)

    HALF = BLOCK // 2
    parts = (0, 1)
    part_lanes = (slice(0, SIDE + 1024), slice(SIDE + 1024, ROW_WIDTH))
    widths = (SIDE + 1024, 1024)

    def cut(part, buffer, *index):
        return buffer.at[(part, *index, slice(None), slice(0, widths[part]))]

    half_lane = lax.broadcasted_iota(jnp.int32, (HALF, SIDE), 1)

    def rounded(part, total):
        if part == 1:
            return total.astype(BF16)
        whole = total[:, 0:SIDE]
        whole = whole + pltpu.roll(whole, SIDE - CYCLES_HERE, 1)
        high = whole.astype(BF16).astype(F32)
        low = pltpu.roll(whole - high, CYCLES_HERE, 1)
        side = jnp.where(half_lane < CYCLES_HERE, high, jnp.where(half_lane < 2 * CYCLES_HERE, low, 0.0))
        return jnp.concatenate([side, total[:, SIDE:]], axis=1).astype(BF16)

    for part in parts:
        out_buf, in_buf = cut(part, core_out), cut(part, core_in)
        for d in range(NX):
            out_buf[d * BLOCK : (d + 1) * BLOCK, :] = sums[class_rows(d, other), part_lanes[part]]
        send(out_buf, in_buf, cs.at[part], cr.at[part], sibling)

    def core_sum(part, x_to, half):
        start = pl.multiple_of(x_to * BLOCK + half * HALF, HALF)
        return (
            sums[half_rows(x_to, core, half), part_lanes[part]]
            + core_in[part, pl.ds(start, HALF), 0 : widths[part]]
        )

    for part in parts:
        remote(
            cut(part, core_out), cut(part, core_in), cs.at[part], cr.at[part], sibling
        ).wait_recv()
        for way in range(2):
            far = cut(part, xfar_out, way)
            far[...] = rounded(part, core_sum(part, (x + 2) % NX, way))
            send(
                far, cut(part, xfar_in, way), xfs.at[part, way], xfr.at[part, way],
                x_peer(steps[way]),
            )
        for way in range(2):
            near = cut(part, xnear_out, way, 1 - way)
            near[...] = rounded(part, core_sum(part, (x + steps[way]) % NX, 1 - way))
            send(
                near, cut(part, xnear_in, way, 1 - way),
                xns.at[part, way, 1 - way], xnr.at[part, way, 1 - way], x_peer(steps[way]),
            )

    for part in parts:
        for way in range(2):
            far = cut(part, xfar_in, way)
            remote(
                cut(part, xfar_out, way), far, xfs.at[part, way], xfr.at[part, way],
                x_peer(steps[way]),
            ).wait_recv()
            near = cut(part, xnear_out, way, way)
            near[...] = rounded(
                part, core_sum(part, (x + steps[way]) % NX, way) + far[...].astype(F32)
            )
            send(
                near, cut(part, xnear_in, way, way),
                xns.at[part, way, way], xnr.at[part, way, way], x_peer(steps[way]),
            )

    for part in parts:
        for half in range(2):
            total = core_sum(part, x, half)
            for way in range(2):
                near = cut(part, xnear_in, way, half)
                remote(
                    cut(part, xnear_out, way, half), near,
                    xns.at[part, way, half], xnr.at[part, way, half], x_peer(steps[way]),
                ).wait_recv()
                total += near[...].astype(F32)
            out_buf = cut(part, rep_out, half)
            out_buf[...] = rounded(part, total)
            send(
                out_buf, cut(part, rep_via, half),
                p1s.at[part, half], p1r.at[part, half], via[half],
            )

    for part in parts:
        for half in range(2):
            via_buf = cut(part, rep_via, half)
            remote(
                cut(part, rep_out, half), via_buf,
                p1s.at[part, half], p1r.at[part, half], via[half],
            ).wait_recv()
            send(
                via_buf, cut(part, rep_in, half), p2s.at[part, half], p2r.at[part, half], via[half]
            )

    density = None
    for part in parts:
        halves = []
        for half in range(2):
            in_buf = cut(part, rep_in, half)
            remote(
                cut(part, rep_via, half), in_buf,
                p2s.at[part, half], p2r.at[part, half], via[half],
            ).wait_recv()
            halves.append(cut(part, rep_out, half)[...].astype(F32) + in_buf[...].astype(F32))
        total = jnp.concatenate(halves, axis=0)
        if part == 0:
            density = total[:, 0:SIDE]
            total = total[:, SIDE:]
        flipped = []
        for n in range(2):
            r = part * 2 + n
            whole = density[:, r : r + 1] + density[:, r + 4 : r + 5]
            piece = total[:, n * 512 : (n + 1) * 512] / (whole + PRIOR_WEIGHT)
            flipped.append(jnp.concatenate([piece[:, 0:256], -piece[:, 256:512]], axis=1))
        result = dft(jnp.concatenate(flipped, axis=0), high_ref, low_ref)
        for n in range(2):
            for p in range(2):
                for h in range(2):
                    lanes = slice(p * 256 + h * 128, p * 256 + h * 128 + 128)
                    piece = result[n * BLOCK : (n + 1) * BLOCK, lanes]
                    start = (part * 2 + n) * 4 + h * 2 + p
                    padded[pl.ds(start, BLOCK, stride=16), :] = piece if p == 0 else -piece
    out_ref[...] = padded[0 : CLASSES_HERE * 16, :]

    for copy in sent:
        copy.wait_send()

    def drain(step, carry):
        for way in range(2):
            piece = near_out.at[step, way]
            remote(piece, piece, fs.at[step, way], fr.at[step, way], z_pair).wait_send()
            for half in range(2):
                remote(
                    piece, piece, ns.at[step, way, half], nr.at[step, way, half], z_pair
                ).wait_send()
            rows = weights.at[0:Y_ROWS, :]
            remote(rows, rows, wys.at[step, way], wyr.at[step, way], z_pair).wait_send()
            half = weights.at[0:PAIR_ROWS, :]
            remote(half, half, wfs.at[step, way], wfr.at[step, way], z_pair).wait_send()

        @pl.when(step < GROUPS - 1)
        def _():
            remote(z_out.at[step], z_in.at[step], zs.at[step], zr.at[step], z_pair).wait_send()

        return carry

    lax.fori_loop(0, GROUPS, drain, 0)


def to_rows(values):
    count = values.shape[0]
    return values.reshape(count, CYCLES_HERE, 2, 2, 128).transpose(0, 1, 3, 2, 4).reshape(count * 16, 128)


def from_rows(rows):
    return (
        rows.reshape(CLASSES_HERE, CYCLES_HERE, 2, 2, 128)
        .transpose(0, 1, 3, 2, 4)
        .reshape(CLASSES_HERE, CYCLES_HERE, 2, 256)
    )


def per_device(particles, references, ctf_table, defocus_ids, rotation_ids):
    vmem = pl.BlockSpec(memory_space=pltpu.VMEM)
    dma = pltpu.SemaphoreType.DMA
    out = pl.pallas_call(
        body,
        out_shape=jax.ShapeDtypeStruct((CLASSES_HERE * 16, 128), F32),
        in_specs=[pl.BlockSpec(memory_space=pl.ANY)] * 7,
        out_specs=vmem,
        scratch_shapes=[
            pltpu.VMEM((PARTICLES_HERE * 16, 128), F32),
            pltpu.VMEM((CLASSES_HERE * 16, 128), F32),
            pltpu.VMEM((512, 512), F32),
            pltpu.VMEM((ALL_CLASSES, ALL_CLASSES), F32),
            pltpu.VMEM((CYCLES_HERE, DEFOCI), F32),
            pltpu.VMEM((1, PARTICLES_HERE), jnp.int32),
            pltpu.VMEM((1, ANGLES), jnp.int32),
            pltpu.VMEM((512, 512), BF16),
            pltpu.VMEM((512, 512), BF16),
            pltpu.VMEM((ALL_CLASSES, ALL_CLASSES), BF16),
            pltpu.VMEM((DEFOCI, 128), F32),
            pltpu.VMEM((2 * TURN_ROWS, SAMPLES), F32),
            pltpu.VMEM((BLOCK * 16, 128), F32),
            pltpu.VMEM((CYCLES_HERE * PARTICLES_HERE, 512), F32),
            pltpu.VMEM((CYCLES_HERE * BLOCK, 512), F32),
            pltpu.VMEM((ALL_CLASSES, ROW_WIDTH), BF16),
            pltpu.VMEM((PARTICLES_HERE, ROW_WIDTH - SIDE), F32),
            pltpu.VMEM((PARTICLES_HERE, 128), F32),
            pltpu.VMEM((4, PARTICLES_HERE, ALL_CLASSES), F32),
            pltpu.VMEM((ALL_ROWS, ROW_WIDTH), BF16),
            pltpu.VMEM((GROUP_ROWS, ALL_CLASSES), F32),
            pltpu.VMEM((ALL_ROWS, ALL_CLASSES), BF16),
            pltpu.VMEM((GROUPS, 2, PAIR_ROWS, ALL_CLASSES), BF16),
            pltpu.VMEM((GROUPS, 2, 2, PAIR_ROWS, ALL_CLASSES), BF16),
            pltpu.VMEM((GROUPS, 2, PAIR_ROWS, ALL_CLASSES), BF16),
            pltpu.VMEM((GROUPS, Y_ROWS, ALL_CLASSES), BF16),
            pltpu.VMEM((GROUPS - 1, Y_ROWS, ALL_CLASSES), BF16),
            pltpu.VMEM((Y_ROWS, ALL_CLASSES), F32),
            pltpu.VMEM((PAIR_ROWS, ALL_CLASSES), BF16),
            pltpu.VMEM((PAIR_ROWS, ALL_CLASSES), BF16),
            pltpu.VMEM((ALL_ROWS, ALL_CLASSES), BF16),
            pltpu.VMEM((ALL_CLASSES, ROW_WIDTH), F32),
            pltpu.VMEM((2, NX * BLOCK, SIDE + 1024), F32),
            pltpu.VMEM((2, NX * BLOCK, SIDE + 1024), F32),
            pltpu.VMEM((2, 2, BLOCK // 2, SIDE + 1024), BF16),
            pltpu.VMEM((2, 2, BLOCK // 2, SIDE + 1024), BF16),
            pltpu.VMEM((2, 2, 2, BLOCK // 2, SIDE + 1024), BF16),
            pltpu.VMEM((2, 2, 2, BLOCK // 2, SIDE + 1024), BF16),
            pltpu.VMEM((2, 2, BLOCK // 2, SIDE + 1024), BF16),
            pltpu.VMEM((2, 2, BLOCK // 2, SIDE + 1024), BF16),
            pltpu.VMEM((2, 2, BLOCK // 2, SIDE + 1024), BF16),
            dma((7,)),
            dma((2,)), dma((2,)), dma((2,)), dma((2,)),
            dma((NX,)), dma((NX,)),
            dma((GROUPS, 2)), dma((GROUPS, 2)),
            dma((GROUPS, 2, 2)), dma((GROUPS, 2, 2)),
            dma((GROUPS - 1,)), dma((GROUPS - 1,)),
            dma(()), dma(()), dma(()), dma(()),
            dma((GROUPS,)), dma((GROUPS,)),
            dma((GROUPS, 2)), dma((GROUPS, 2)),
            dma((GROUPS, 2)), dma((GROUPS, 2)),
            dma((2,)), dma((2,)),
            dma((2, 2)), dma((2, 2)),
            dma((2, 2, 2)), dma((2, 2, 2)),
            dma((2, 2)), dma((2, 2)), dma((2, 2)), dma((2, 2)),
        ],
        compiler_params=pltpu.CompilerParams(
            collective_id=0, has_side_effects=True, vmem_limit_bytes=56 * 1024 * 1024
        ),
    )(
        to_rows(particles), to_rows(references), jnp.asarray(dft_matrix()), jnp.asarray(walsh_matrix()),
        ctf_table.T, defocus_ids.reshape(1, PARTICLES_HERE), rotation_ids.reshape(1, ANGLES),
    )
    return from_rows(out)


def solution(mesh):
    in_specs = (
        P(("cls", "rep"), "pix", None, None),
        P("cls", "pix", None, None),
        P(None, "pix"),
        P(("cls", "rep")),
        P(),
    )
    out_specs = P("cls", "pix", None, None)
    return jax.shard_map(
        per_device, mesh=mesh, in_specs=in_specs, out_specs=out_specs, check_vma=False
    )
```

time: 880 us -> 104 us (0.12)
  blocking collectives: 338 us -> 0 us
  waiting for transfers between devices: 282 us -> 0 us
  Pallas kernels: 0 us -> 102 us
  other arithmetic: 94.8 us -> 0 us
  local copies, waits for them, and re-layouts: 65.4 us -> 1.62 us
  matrix products: 41.1 us -> 0 us
  loops' own time: 36.2 us -> 0 us
  between operations: 14.4 us -> 0.01 us
    psum x2 -> x0, waiting for transfers between devices: 282 us -> none  [the longest x1 221 us: per_device(): lax.psum((products, part_norm, ref_norm), 'pix')]
    psum x2 -> x0, blocking collectives: 277 us -> none  [the longest x1 207 us: per_device(): lax.psum((products, part_norm, ref_norm), 'pix')]
    pallas_call x0 -> x1, Pallas kernels: none -> 102 us  [per_device(): pl.pallas_call(body, out_shape=jax.ShapeDtypeStruct((CLASSES_HERE * 16, 1...]
    another operation x36 -> x0, other arithmetic: 83.6 us -> none  [the longest x18 43.8 us: turned_rows(): stacked = jnp.stack([turned_re, turned_im], axis=3).astype(jnp.bfloat16)]
    dot_general x25 -> x0, matrix products: 41.1 us -> none  [the longest x9 26 us: class_angle_step(): lax.dot_general(picked, rows_now, (((0,), (0,)), ((), ())), preferred_ele...]
    unnamed x1 -> x0, blocking collectives: 40.6 us -> none
    another operation x2 -> x0, loops' own time: 36.2 us -> none  [the longest x1 18.8 us: class_sums(): lax.scan(class_angle_step, jnp.zeros((class_count, row_width), jnp.float3...]
    dynamic_slice x45 -> x0, local copies, waits for them, and re-layouts: 26.3 us -> none  [the longest x18 11.4 us: correlate_all(): lax.scan(correlate_angle_step, jnp.zeros((), jnp.int32), firsts)[1]]
  transfers between devices with their start and end apart: 4 -> 0, of which waited for: 2 -> 0; matrix products, arithmetic and copies ran while one was open for 1% -> 0% of each run, Pallas kernels for 0% -> 0%
where the time goes in v1:
time: 104 us
  Pallas kernels  102 us (98%)
  local copies, waits for them, and re-layouts  1.62 us (2%)
    pallas_call x1, Pallas kernels, per_device(): pl.pallas_call(body, out_shape=jax.ShapeDtypeStruct((CLASSES_HERE * 16, 1...  102 us

profile of v1, /device:TPU:1, one launch (start us, length us, event | category | flops | bytes accessed | tf_op | source)
XLA Modules:
  0.0 103.6 jit_solution(15123870790037475505)
XLA Ops:
  0.0 102.0 %shard_map.73 = f32[400,128]{1,0:T(8,128)} custom-call(f32[1024,128]{1,0:T(8,128)} %bitcast.19, f32[400,128]{1,0:T(8,128)} %bitcast.20, f32[512,512]{1,0:T(8,128)} %constant.4.clone.dft_hbm, f32[256,256]{1,0:T(8,128)} %constant.5.clone.walsh_hbm, f32[4,16]{1,0:T(4,128)} %bitcast.21, s32[1,64]{1,0:T(1,128)} %bitcast.22, s32[1,36]{1,0:T(1,128)} %bitcast.23), custom_call_target="tpu_custom_call" | custom-call | tf_op jit(solution)/shard_map/pallas_call | solution.py:671
  102.0 1.6 %copy.12 = f32[25,4,2,256]{3,2,1,0:T(2,128)} copy(f32[25,4,2,256]{3,2,1,0:T(2,128)} %bitcast.18) | data formatting | bytes 409600

commit v2 on v1

--- a/solution.py
+++ b/solution.py
@@ -81,10 +81,10 @@
     x_ref, r_ref, dft_ref, walsh_f, ctf_in, ids_ref, turns_ref,
     high_ref, low_ref, walsh_ref, ctf_ref, phase_ref,
     padded, x_rows, r_rows, spectra, weighted, power_rows, norm_rows, turned,
-    partial_f, partial, far_in, near_in, near_out, z_out, z_in, z_sum, pair_out, pair_in, weights,
+    partial_f, partial, far_in, near_in, near_out, z_out, z_in, pair_out, pair_in, weights,
     sums, core_out, core_in, xfar_out, xfar_in, xnear_out, xnear_in, rep_out, rep_via, rep_in,
     in_sem, rx_s, rx_r, rf_s, rf_r, rc_s, rc_r,
-    fs, fr, ns, nr, zs, zr, zps, zpr, wps, wpr, wzs, wzr, wys, wyr, wfs, wfr,
+    fs, fr, ns, nr, zs, zr, zps, zpr, wzs, wzr, wys, wyr, wfs, wfr,
     cs, cr, xfs, xfr, xns, xnr, p1s, p1r, p2s, p2r,
 ):
     loads = [
@@ -413,15 +413,13 @@
     for n in range(GROUPS - 1):
         remote(z_out.at[n], z_in.at[n], zs.at[n], zr.at[n], z_pair).wait_recv()
         total += z_in[n].astype(F32)
-    z_sum[...] = total
-    pair_out[...] = product_rounded(
-        z_sum[pl.ds(pl.multiple_of((1 - zh) * PAIR_ROWS, 16), PAIR_ROWS), :]
-    )
+    for half in range(2):
+        rows = slice(half * PAIR_ROWS, (half + 1) * PAIR_ROWS)
+        pair_out[rows, :] = product_rounded(total[rows, :])
     send(pair_out, pair_in, zps, zpr, z_pair)
-    mine = z_sum[pl.ds(pl.multiple_of(zh * PAIR_ROWS, 16), PAIR_ROWS), :]
     sums[...] = jnp.zeros_like(sums)
     remote(pair_out, pair_in, zps, zpr, z_pair).wait_recv()
-    mine += pair_in[...].astype(F32)
+    mine = total + pair_in[...].astype(F32)
 
     shape = (TURN_ROWS, ALL_CLASSES)
     valid = (lax.broadcasted_iota(jnp.int32, shape, 0) < ANGLES) & (
@@ -429,7 +427,7 @@
     )
     products = walsh(mine, walsh_ref) * (1.0 / ALL_CLASSES)
     pieces = []
-    for e in range(2):
+    for e in range(4):
         rows = mine[e * TURN_ROWS : (e + 1) * TURN_ROWS, :]
         ref_row = rows[36:37, :] + rows[37:38, :]
         part_row = rows[38:39, :] + rows[39:40, :]
@@ -441,12 +439,8 @@
         total = jnp.sum(jnp.sum(raised, axis=0, keepdims=True), axis=1, keepdims=True)
         pieces.append(raised / total)
 
-    own_pair = weights.at[y_half_of(q, y, zh), :]
-    own_pair[...] = jnp.concatenate(pieces, axis=0).astype(BF16)
-    send(own_pair, own_pair, wps, wpr, z_pair)
-    pair = weights.at[y_half_of(q, y, 1 - zh), :]
-    remote(pair, pair, wps, wpr, z_pair).wait_recv()
     group_rows = weights.at[y_rows_of(q, y), :]
+    group_rows[...] = jnp.concatenate(pieces, axis=0).astype(BF16)
     for d in (1, 3, 2):
         send(group_rows, group_rows, wzs.at[d], wzr.at[d], q_peer((q + d) % 4))
 
@@ -509,12 +503,11 @@
     def cut(part, buffer, *index):
         return buffer.at[(part, *index, slice(None), slice(0, widths[part]))]
 
-    half_lane = lax.broadcasted_iota(jnp.int32, (HALF, SIDE), 1)
-
     def rounded(part, total):
         if part == 1:
             return total.astype(BF16)
         whole = total[:, 0:SIDE]
+        half_lane = lax.broadcasted_iota(jnp.int32, whole.shape, 1)
         whole = whole + pltpu.roll(whole, SIDE - CYCLES_HERE, 1)
         high = whole.astype(BF16).astype(F32)
         low = pltpu.roll(whole - high, CYCLES_HERE, 1)
@@ -524,14 +517,16 @@
     for part in parts:
         out_buf, in_buf = cut(part, core_out), cut(part, core_in)
         for d in range(NX):
-            out_buf[d * BLOCK : (d + 1) * BLOCK, :] = sums[class_rows(d, other), part_lanes[part]]
+            out_buf[d * BLOCK : (d + 1) * BLOCK, :] = rounded(
+                part, sums[class_rows(d, other), part_lanes[part]]
+            )
         send(out_buf, in_buf, cs.at[part], cr.at[part], sibling)
 
     def core_sum(part, x_to, half):
         start = pl.multiple_of(x_to * BLOCK + half * HALF, HALF)
         return (
             sums[half_rows(x_to, core, half), part_lanes[part]]
-            + core_in[part, pl.ds(start, HALF), 0 : widths[part]]
+            + core_in[part, pl.ds(start, HALF), 0 : widths[part]].astype(F32)
         )
 
     for part in parts:
@@ -701,13 +696,12 @@
             pltpu.VMEM((GROUPS, 2, PAIR_ROWS, ALL_CLASSES), BF16),
             pltpu.VMEM((GROUPS, Y_ROWS, ALL_CLASSES), BF16),
             pltpu.VMEM((GROUPS - 1, Y_ROWS, ALL_CLASSES), BF16),
-            pltpu.VMEM((Y_ROWS, ALL_CLASSES), F32),
-            pltpu.VMEM((PAIR_ROWS, ALL_CLASSES), BF16),
-            pltpu.VMEM((PAIR_ROWS, ALL_CLASSES), BF16),
+            pltpu.VMEM((Y_ROWS, ALL_CLASSES), BF16),
+            pltpu.VMEM((Y_ROWS, ALL_CLASSES), BF16),
             pltpu.VMEM((ALL_ROWS, ALL_CLASSES), BF16),
             pltpu.VMEM((ALL_CLASSES, ROW_WIDTH), F32),
-            pltpu.VMEM((2, NX * BLOCK, SIDE + 1024), F32),
-            pltpu.VMEM((2, NX * BLOCK, SIDE + 1024), F32),
+            pltpu.VMEM((2, NX * BLOCK, SIDE + 1024), BF16),
+            pltpu.VMEM((2, NX * BLOCK, SIDE + 1024), BF16),
             pltpu.VMEM((2, 2, BLOCK // 2, SIDE + 1024), BF16),
             pltpu.VMEM((2, 2, BLOCK // 2, SIDE + 1024), BF16),
             pltpu.VMEM((2, 2, 2, BLOCK // 2, SIDE + 1024), BF16),
@@ -721,7 +715,7 @@
             dma((GROUPS, 2)), dma((GROUPS, 2)),
             dma((GROUPS, 2, 2)), dma((GROUPS, 2, 2)),
             dma((GROUPS - 1,)), dma((GROUPS - 1,)),
-            dma(()), dma(()), dma(()), dma(()),
+            dma(()), dma(()),
             dma((GROUPS,)), dma((GROUPS,)),
             dma((GROUPS, 2)), dma((GROUPS, 2)),
             dma((GROUPS, 2)), dma((GROUPS, 2)),

time: 104 us -> 103 us (level)
  the two profiles are of different devices: /device:TPU:1 before, /device:TPU:35 now
where the time goes in v2:
time: 103 us
  Pallas kernels  101 us (98%)
  local copies, waits for them, and re-layouts  1.62 us (2%)
    pallas_call x1, Pallas kernels, per_device(): pl.pallas_call(body, out_shape=jax.ShapeDtypeStruct((CLASSES_HERE * 16, 1...  101 us

profile of v2, /device:TPU:35, one launch (start us, length us, event | category | flops | bytes accessed | tf_op | source)
XLA Modules:
  0.0 103.0 jit_solution(7875404889751896596)
XLA Ops:
  0.0 101.3 %shard_map.73 = f32[400,128]{1,0:T(8,128)} custom-call(f32[1024,128]{1,0:T(8,128)} %bitcast.19, f32[400,128]{1,0:T(8,128)} %bitcast.20, f32[512,512]{1,0:T(8,128)} %constant.4.clone.dft_hbm, f32[256,256]{1,0:T(8,128)} %constant.5.clone.walsh_hbm, f32[4,16]{1,0:T(4,128)} %bitcast.21, s32[1,64]{1,0:T(1,128)} %bitcast.22, s32[1,36]{1,0:T(1,128)} %bitcast.23), custom_call_target="tpu_custom_call" | custom-call | tf_op jit(solution)/shard_map/pallas_call | solution.py:666
  101.3 1.6 %copy.12 = f32[25,4,2,256]{3,2,1,0:T(2,128)} copy(f32[25,4,2,256]{3,2,1,0:T(2,128)} %bitcast.18) | data formatting | bytes 409600

commit v3 on v2

--- a/solution.py
+++ b/solution.py
@@ -346,12 +346,6 @@
                 partial.at[y_half_of(group, (y + 2) % NY, way), :],
                 far_in.at[step, way], fs.at[step, way], fr.at[step, way], y_peer(steps[way]),
             )
-        for way in range(2):
-            start_copy(
-                partial.at[y_half_of(group, (y + steps[way]) % NY, 1 - way), :],
-                near_in.at[step, way, 1 - way],
-                ns.at[step, way, 1 - way], nr.at[step, way, 1 - way], y_peer(steps[way]),
-            )
 
     odd_row = sub % 2 == 1
 
@@ -374,24 +368,27 @@
             remote(
                 own, far_in.at[step, way], fs.at[step, way], fr.at[step, way], y_peer(steps[way])
             ).wait_recv()
-            near_out[step, way] = product_rounded(
+            near_out[step, way, way] = product_rounded(
                 own[...].astype(F32) + far_in[step, way].astype(F32)
             )
+            near_out[step, way, 1 - way] = partial[
+                y_half_of(group, (y + steps[way]) % NY, 1 - way), :
+            ]
             start_copy(
-                near_out.at[step, way], near_in.at[step, way, way],
-                ns.at[step, way, way], nr.at[step, way, way], y_peer(steps[way]),
+                near_out.at[step, way], near_in.at[step, way],
+                ns.at[step, way], nr.at[step, way], y_peer(steps[way]),
             )
 
     def reduce_y(step):
         group = z_group(step)
+        for way in range(2):
+            remote(
+                near_out.at[step, way], near_in.at[step, way],
+                ns.at[step, way], nr.at[step, way], y_peer(steps[way]),
+            ).wait_recv()
         for half in range(2):
-            own = partial.at[y_half_of(group, y, half), :]
-            total = own[...].astype(F32)
+            total = partial[y_half_of(group, y, half), :].astype(F32)
             for way in range(2):
-                remote(
-                    own, near_in.at[step, way, half],
-                    ns.at[step, way, half], nr.at[step, way, half], y_peer(steps[way]),
-                ).wait_recv()
                 total += near_in[step, way, half].astype(F32)
             z_out[step, half * PAIR_ROWS : (half + 1) * PAIR_ROWS, :] = product_rounded(total)
 
@@ -469,20 +466,20 @@
             half = weights.at[y_half_of(group, y_of, way), :]
             start_copy(half, half, wfs.at[step, way], wfr.at[step, way], y_peer(steps[way]))
 
-    def add_group(step):
+    def await_group(step):
         group = w_group(step)
         for way in range(2):
             half = weights.at[y_half_of(group, (y + 2) % NY, way), :]
             remote(
                 half, half, wfs.at[step, way], wfr.at[step, way], y_peer(steps[way])
             ).wait_recv()
-        rows = pl.ds(pl.multiple_of(group * GROUP_ROWS, GROUP_ROWS), GROUP_ROWS)
+        return pl.ds(pl.multiple_of(group * GROUP_ROWS, GROUP_ROWS), GROUP_ROWS)
+
+    def add_group(step):
+        rows = await_group(step)
         picked_weights = weights[rows, :].T
-        sums[:, 0:SIDE] += lax.dot_general(
-            picked_weights, turned[rows, 0:SIDE], NN, preferred_element_type=F32
-        )
         for r in range(CYCLES_HERE):
-            lanes = slice(SIDE + r * 512, SIDE + (r + 1) * 512)
+            lanes = slice(SIDE + r * 512 if r else 0, SIDE + (r + 1) * 512)
             sums[:, lanes] += lax.dot_general(
                 picked_weights, turned[rows, lanes], NN, preferred_element_type=F32
             )
@@ -496,130 +493,78 @@
     lax.fori_loop(0, GROUPS + 2, weight_step, 0)
 
     HALF = BLOCK // 2
-    parts = (0, 1)
-    part_lanes = (slice(0, SIDE + 1024), slice(SIDE + 1024, ROW_WIDTH))
-    widths = (SIDE + 1024, 1024)
-
-    def cut(part, buffer, *index):
-        return buffer.at[(part, *index, slice(None), slice(0, widths[part]))]
-
-    def rounded(part, total):
-        if part == 1:
-            return total.astype(BF16)
+    def rounded(total):
         whole = total[:, 0:SIDE]
-        half_lane = lax.broadcasted_iota(jnp.int32, whole.shape, 1)
+        side_lane = lax.broadcasted_iota(jnp.int32, whole.shape, 1)
         whole = whole + pltpu.roll(whole, SIDE - CYCLES_HERE, 1)
         high = whole.astype(BF16).astype(F32)
         low = pltpu.roll(whole - high, CYCLES_HERE, 1)
-        side = jnp.where(half_lane < CYCLES_HERE, high, jnp.where(half_lane < 2 * CYCLES_HERE, low, 0.0))
+        side = jnp.where(side_lane < CYCLES_HERE, high, jnp.where(side_lane < 2 * CYCLES_HERE, low, 0.0))
         return jnp.concatenate([side, total[:, SIDE:]], axis=1).astype(BF16)
 
-    for part in parts:
-        out_buf, in_buf = cut(part, core_out), cut(part, core_in)
-        for d in range(NX):
-            out_buf[d * BLOCK : (d + 1) * BLOCK, :] = rounded(
-                part, sums[class_rows(d, other), part_lanes[part]]
-            )
-        send(out_buf, in_buf, cs.at[part], cr.at[part], sibling)
-
-    def core_sum(part, x_to, half):
+    def core_block(d, carry):
+        core_out[pl.ds(pl.multiple_of(d * BLOCK, BLOCK), BLOCK), :] = rounded(
+            sums[class_rows(d, other), :]
+        )
+        return carry
+
+    lax.fori_loop(0, NX, core_block, 0)
+    send(core_out, core_in, cs, cr, sibling)
+
+    def core_sum(x_to, half):
         start = pl.multiple_of(x_to * BLOCK + half * HALF, HALF)
-        return (
-            sums[half_rows(x_to, core, half), part_lanes[part]]
-            + core_in[part, pl.ds(start, HALF), 0 : widths[part]].astype(F32)
-        )
-
-    for part in parts:
+        return sums[half_rows(x_to, core, half), :] + core_in[pl.ds(start, HALF), :].astype(F32)
+
+    remote(core_out, core_in, cs, cr, sibling).wait_recv()
+    for way in range(2):
+        xfar_out[way] = rounded(core_sum((x + 2) % NX, way))
+        send(xfar_out.at[way], xfar_in.at[way], xfs.at[way], xfr.at[way], x_peer(steps[way]))
+    for way in range(2):
+        xnear_out[way, 1 - way] = rounded(core_sum((x + steps[way]) % NX, 1 - way))
+    for way in range(2):
         remote(
-            cut(part, core_out), cut(part, core_in), cs.at[part], cr.at[part], sibling
+            xfar_out.at[way], xfar_in.at[way], xfs.at[way], xfr.at[way], x_peer(steps[way])
         ).wait_recv()
-        for way in range(2):
-            far = cut(part, xfar_out, way)
-            far[...] = rounded(part, core_sum(part, (x + 2) % NX, way))
-            send(
-                far, cut(part, xfar_in, way), xfs.at[part, way], xfr.at[part, way],
-                x_peer(steps[way]),
-            )
-        for way in range(2):
-            near = cut(part, xnear_out, way, 1 - way)
-            near[...] = rounded(part, core_sum(part, (x + steps[way]) % NX, 1 - way))
-            send(
-                near, cut(part, xnear_in, way, 1 - way),
-                xns.at[part, way, 1 - way], xnr.at[part, way, 1 - way], x_peer(steps[way]),
-            )
-
-    for part in parts:
-        for way in range(2):
-            far = cut(part, xfar_in, way)
-            remote(
-                cut(part, xfar_out, way), far, xfs.at[part, way], xfr.at[part, way],
-                x_peer(steps[way]),
-            ).wait_recv()
-            near = cut(part, xnear_out, way, way)
-            near[...] = rounded(
-                part, core_sum(part, (x + steps[way]) % NX, way) + far[...].astype(F32)
-            )
-            send(
-                near, cut(part, xnear_in, way, way),
-                xns.at[part, way, way], xnr.at[part, way, way], x_peer(steps[way]),
-            )
-
-    for part in parts:
-        for half in range(2):
-            total = core_sum(part, x, half)
-            for way in range(2):
-                near = cut(part, xnear_in, way, half)
-                remote(
-                    cut(part, xnear_out, way, half), near,
-                    xns.at[part, way, half], xnr.at[part, way, half], x_peer(steps[way]),
-                ).wait_recv()
-                total += near[...].astype(F32)
-            out_buf = cut(part, rep_out, half)
-            out_buf[...] = rounded(part, total)
-            send(
-                out_buf, cut(part, rep_via, half),
-                p1s.at[part, half], p1r.at[part, half], via[half],
-            )
-
-    for part in parts:
-        for half in range(2):
-            via_buf = cut(part, rep_via, half)
-            remote(
-                cut(part, rep_out, half), via_buf,
-                p1s.at[part, half], p1r.at[part, half], via[half],
-            ).wait_recv()
-            send(
-                via_buf, cut(part, rep_in, half), p2s.at[part, half], p2r.at[part, half], via[half]
-            )
-
-    density = None
-    for part in parts:
-        halves = []
-        for half in range(2):
-            in_buf = cut(part, rep_in, half)
-            remote(
-                cut(part, rep_via, half), in_buf,
-                p2s.at[part, half], p2r.at[part, half], via[half],
-            ).wait_recv()
-            halves.append(cut(part, rep_out, half)[...].astype(F32) + in_buf[...].astype(F32))
-        total = jnp.concatenate(halves, axis=0)
-        if part == 0:
-            density = total[:, 0:SIDE]
-            total = total[:, SIDE:]
-        flipped = []
-        for n in range(2):
-            r = part * 2 + n
-            whole = density[:, r : r + 1] + density[:, r + 4 : r + 5]
-            piece = total[:, n * 512 : (n + 1) * 512] / (whole + PRIOR_WEIGHT)
-            flipped.append(jnp.concatenate([piece[:, 0:256], -piece[:, 256:512]], axis=1))
-        result = dft(jnp.concatenate(flipped, axis=0), high_ref, low_ref)
-        for n in range(2):
-            for p in range(2):
-                for h in range(2):
-                    lanes = slice(p * 256 + h * 128, p * 256 + h * 128 + 128)
-                    piece = result[n * BLOCK : (n + 1) * BLOCK, lanes]
-                    start = (part * 2 + n) * 4 + h * 2 + p
-                    padded[pl.ds(start, BLOCK, stride=16), :] = piece if p == 0 else -piece
+        xnear_out[way, way] = rounded(
+            core_sum((x + steps[way]) % NX, way) + xfar_in[way].astype(F32)
+        )
+        send(xnear_out.at[way], xnear_in.at[way], xns.at[way], xnr.at[way], x_peer(steps[way]))
+    for way in range(2):
+        remote(
+            xnear_out.at[way], xnear_in.at[way], xns.at[way], xnr.at[way], x_peer(steps[way])
+        ).wait_recv()
+
+    for half in range(2):
+        total = core_sum(x, half)
+        for way in range(2):
+            total += xnear_in[way, half].astype(F32)
+        rep_out[half] = rounded(total)
+        send(rep_out.at[half], rep_via.at[half], p1s.at[half], p1r.at[half], via[half])
+    for half in range(2):
+        remote(
+            rep_out.at[half], rep_via.at[half], p1s.at[half], p1r.at[half], via[half]
+        ).wait_recv()
+        send(rep_via.at[half], rep_in.at[half], p2s.at[half], p2r.at[half], via[half])
+    halves = []
+    for half in range(2):
+        remote(
+            rep_via.at[half], rep_in.at[half], p2s.at[half], p2r.at[half], via[half]
+        ).wait_recv()
+        halves.append(rep_out[half].astype(F32) + rep_in[half].astype(F32))
+    total = jnp.concatenate(halves, axis=0)
+    for r in range(CYCLES_HERE):
+        density = total[:, r : r + 1] + total[:, r + CYCLES_HERE : r + CYCLES_HERE + 1]
+        piece = total[:, SIDE + r * 512 : SIDE + (r + 1) * 512] / (density + PRIOR_WEIGHT)
+        r_rows[r * BLOCK : (r + 1) * BLOCK, 0:256] = piece[:, 0:256]
+        r_rows[r * BLOCK : (r + 1) * BLOCK, 256:512] = -piece[:, 256:512]
+    result = dft(r_rows[...], high_ref, low_ref)
+    for r in range(CYCLES_HERE):
+        for p in range(2):
+            for h in range(2):
+                piece = result[
+                    r * BLOCK : (r + 1) * BLOCK, p * 256 + h * 128 : p * 256 + h * 128 + 128
+                ]
+                padded[pl.ds(r * 4 + h * 2 + p, BLOCK, stride=16), :] = piece if p == 0 else -piece
     out_ref[...] = padded[0 : CLASSES_HERE * 16, :]
 
     for copy in sent:
@@ -627,12 +572,10 @@
 
     def drain(step, carry):
         for way in range(2):
+            piece = far_in.at[step, way]
+            remote(piece, piece, fs.at[step, way], fr.at[step, way], z_pair).wait_send()
             piece = near_out.at[step, way]
-            remote(piece, piece, fs.at[step, way], fr.at[step, way], z_pair).wait_send()
-            for half in range(2):
-                remote(
-                    piece, piece, ns.at[step, way, half], nr.at[step, way, half], z_pair
-                ).wait_send()
+            remote(piece, piece, ns.at[step, way], nr.at[step, way], z_pair).wait_send()
             rows = weights.at[0:Y_ROWS, :]
             remote(rows, rows, wys.at[step, way], wyr.at[step, way], z_pair).wait_send()
             half = weights.at[0:PAIR_ROWS, :]
@@ -693,36 +636,35 @@
             pltpu.VMEM((ALL_ROWS, ALL_CLASSES), BF16),
             pltpu.VMEM((GROUPS, 2, PAIR_ROWS, ALL_CLASSES), BF16),
             pltpu.VMEM((GROUPS, 2, 2, PAIR_ROWS, ALL_CLASSES), BF16),
-            pltpu.VMEM((GROUPS, 2, PAIR_ROWS, ALL_CLASSES), BF16),
+            pltpu.VMEM((GROUPS, 2, 2, PAIR_ROWS, ALL_CLASSES), BF16),
             pltpu.VMEM((GROUPS, Y_ROWS, ALL_CLASSES), BF16),
             pltpu.VMEM((GROUPS - 1, Y_ROWS, ALL_CLASSES), BF16),
             pltpu.VMEM((Y_ROWS, ALL_CLASSES), BF16),
             pltpu.VMEM((Y_ROWS, ALL_CLASSES), BF16),
             pltpu.VMEM((ALL_ROWS, ALL_CLASSES), BF16),
             pltpu.VMEM((ALL_CLASSES, ROW_WIDTH), F32),
-            pltpu.VMEM((2, NX * BLOCK, SIDE + 1024), BF16),
-            pltpu.VMEM((2, NX * BLOCK, SIDE + 1024), BF16),
-            pltpu.VMEM((2, 2, BLOCK // 2, SIDE + 1024), BF16),
-            pltpu.VMEM((2, 2, BLOCK // 2, SIDE + 1024), BF16),
-            pltpu.VMEM((2, 2, 2, BLOCK // 2, SIDE + 1024), BF16),
-            pltpu.VMEM((2, 2, 2, BLOCK // 2, SIDE + 1024), BF16),
-            pltpu.VMEM((2, 2, BLOCK // 2, SIDE + 1024), BF16),
-            pltpu.VMEM((2, 2, BLOCK // 2, SIDE + 1024), BF16),
-            pltpu.VMEM((2, 2, BLOCK // 2, SIDE + 1024), BF16),
+            pltpu.VMEM((NX * BLOCK, ROW_WIDTH), BF16),
+            pltpu.VMEM((NX * BLOCK, ROW_WIDTH), BF16),
+            pltpu.VMEM((2, BLOCK // 2, ROW_WIDTH), BF16),
+            pltpu.VMEM((2, BLOCK // 2, ROW_WIDTH), BF16),
+            pltpu.VMEM((2, 2, BLOCK // 2, ROW_WIDTH), BF16),
+            pltpu.VMEM((2, 2, BLOCK // 2, ROW_WIDTH), BF16),
+            pltpu.VMEM((2, BLOCK // 2, ROW_WIDTH), BF16),
+            pltpu.VMEM((2, BLOCK // 2, ROW_WIDTH), BF16),
+            pltpu.VMEM((2, BLOCK // 2, ROW_WIDTH), BF16),
             dma((7,)),
             dma((2,)), dma((2,)), dma((2,)), dma((2,)),
             dma((NX,)), dma((NX,)),
             dma((GROUPS, 2)), dma((GROUPS, 2)),
-            dma((GROUPS, 2, 2)), dma((GROUPS, 2, 2)),
+            dma((GROUPS, 2)), dma((GROUPS, 2)),
             dma((GROUPS - 1,)), dma((GROUPS - 1,)),
             dma(()), dma(()),
             dma((GROUPS,)), dma((GROUPS,)),
             dma((GROUPS, 2)), dma((GROUPS, 2)),
             dma((GROUPS, 2)), dma((GROUPS, 2)),
-            dma((2,)), dma((2,)),
-            dma((2, 2)), dma((2, 2)),
-            dma((2, 2, 2)), dma((2, 2, 2)),
-            dma((2, 2)), dma((2, 2)), dma((2, 2)), dma((2, 2)),
+            dma(()), dma(()),
+            dma((2,)), dma((2,)), dma((2,)), dma((2,)),
+            dma((2,)), dma((2,)), dma((2,)), dma((2,)),
         ],
         compiler_params=pltpu.CompilerParams(
             collective_id=0, has_side_effects=True, vmem_limit_bytes=56 * 1024 * 1024

time: 103 us -> 105 us (1.019)
  Pallas kernels: 101 us -> 103 us
    pallas_call x1, Pallas kernels: 101 us -> 103 us  [per_device(): pl.pallas_call(body, out_shape=jax.ShapeDtypeStruct((CLASSES_HERE * 16, 1...]
where the time goes in v3:
time: 105 us
  Pallas kernels  103 us (98%)
  local copies, waits for them, and re-layouts  1.62 us (2%)
    pallas_call x1, Pallas kernels, per_device(): pl.pallas_call(body, out_shape=jax.ShapeDtypeStruct((CLASSES_HERE * 16, 1...  103 us

profile of v3, /device:TPU:35, one launch (start us, length us, event | category | flops | bytes accessed | tf_op | source)
XLA Modules:
  0.0 105.0 jit_solution(5807763841305008287)
XLA Ops:
  0.0 103.3 %shard_map.73 = f32[400,128]{1,0:T(8,128)} custom-call(f32[1024,128]{1,0:T(8,128)} %bitcast.19, f32[400,128]{1,0:T(8,128)} %bitcast.20, f32[512,512]{1,0:T(8,128)} %constant.4.clone.dft_hbm, f32[256,256]{1,0:T(8,128)} %constant.5.clone.walsh_hbm, f32[4,16]{1,0:T(4,128)} %bitcast.21, s32[1,64]{1,0:T(1,128)} %bitcast.22, s32[1,36]{1,0:T(1,128)} %bitcast.23), custom_call_target="tpu_custom_call" | custom-call | tf_op jit(solution)/shard_map/pallas_call | solution.py:609
  103.3 1.6 %copy.12 = f32[25,4,2,256]{3,2,1,0:T(2,128)} copy(f32[25,4,2,256]{3,2,1,0:T(2,128)} %bitcast.18) | data formatting | bytes 409600

commit v4 on v2

--- a/solution.py
+++ b/solution.py
@@ -80,7 +80,7 @@
     x_hbm, r_hbm, dft_hbm, walsh_hbm, ctf_hbm, ids_hbm, turns_hbm, out_ref,
     x_ref, r_ref, dft_ref, walsh_f, ctf_in, ids_ref, turns_ref,
     high_ref, low_ref, walsh_ref, ctf_ref, phase_ref,
-    padded, x_rows, r_rows, spectra, weighted, power_rows, norm_rows, turned,
+    padded, x_rows, r_rows, spectra, mixed, weighted, power_rows, norm_rows, turned,
     partial_f, partial, far_in, near_in, near_out, z_out, z_in, pair_out, pair_in, weights,
     sums, core_out, core_in, xfar_out, xfar_in, xnear_out, xnear_in, rep_out, rep_via, rep_in,
     in_sem, rx_s, rx_r, rf_s, rf_r, rc_s, rc_r,
@@ -293,6 +293,12 @@
         rows = spectra.at[class_rows(x_of, other), :]
         remote(rows, rows, rc_s.at[n], rc_r.at[n], sibling).wait_recv()
 
+    for r in range(CYCLES_HERE):
+        mixed[:, r * 512 : (r + 1) * 512] = lax.dot_general(
+            walsh_ref[...], spectra[:, SIDE + r * 512 : SIDE + (r + 1) * 512], NN,
+            preferred_element_type=F32,
+        ).astype(BF16)
+
     ctf_high, ctf_low = split(ctf_ref[...] * ctf_ref[...])
     ref_norm = lax.dot_general(
         ctf_high, spectra[:, 0:SIDE], NT, preferred_element_type=F32
@@ -322,8 +328,8 @@
     def correlate(step):
         group = z_group(step)
         rows = pl.ds(pl.multiple_of(group * GROUP_ROWS, GROUP_ROWS), GROUP_ROWS)
-        partial_f[...] = walsh(
-            lax.dot_general(turned[rows, SIDE:], spectra[:, SIDE:], NT, preferred_element_type=F32), walsh_ref
+        partial_f[...] = lax.dot_general(
+            turned[rows, SIDE:], mixed[...], NT, preferred_element_type=F32
         )
 
         def patch(pair, carry):
@@ -685,6 +691,7 @@
             pltpu.VMEM((CYCLES_HERE * PARTICLES_HERE, 512), F32),
             pltpu.VMEM((CYCLES_HERE * BLOCK, 512), F32),
             pltpu.VMEM((ALL_CLASSES, ROW_WIDTH), BF16),
+            pltpu.VMEM((ALL_CLASSES, ROW_WIDTH - SIDE), BF16),
             pltpu.VMEM((PARTICLES_HERE, ROW_WIDTH - SIDE), F32),
             pltpu.VMEM((PARTICLES_HERE, 128), F32),
             pltpu.VMEM((4, PARTICLES_HERE, ALL_CLASSES), F32),

time: 103 us -> 102 us (level)
  the two profiles are of different devices: /device:TPU:35 before, /device:TPU:58 now
where the time goes in v4:
time: 102 us
  Pallas kernels  101 us (99%)
  local copies, waits for them, and re-layouts  1.62 us (2%)
    pallas_call x1, Pallas kernels, per_device(): pl.pallas_call(body, out_shape=jax.ShapeDtypeStruct((CLASSES_HERE * 16, 1...  101 us

profile of v4, /device:TPU:58, one launch (start us, length us, event | category | flops | bytes accessed | tf_op | source)
XLA Modules:
  0.0 102.2 jit_solution(16790101887612287678)
XLA Ops:
  0.0 100.6 %shard_map.73 = f32[400,128]{1,0:T(8,128)} custom-call(f32[1024,128]{1,0:T(8,128)} %bitcast.19, f32[400,128]{1,0:T(8,128)} %bitcast.20, f32[512,512]{1,0:T(8,128)} %constant.4.clone.dft_hbm, f32[256,256]{1,0:T(8,128)} %constant.5.clone.walsh_hbm, f32[4,16]{1,0:T(4,128)} %bitcast.21, s32[1,64]{1,0:T(1,128)} %bitcast.22, s32[1,36]{1,0:T(1,128)} %bitcast.23), custom_call_target="tpu_custom_call" | custom-call | tf_op jit(solution)/shard_map/pallas_call | solution.py:672
  100.6 1.6 %copy.12 = f32[25,4,2,256]{3,2,1,0:T(2,128)} copy(f32[25,4,2,256]{3,2,1,0:T(2,128)} %bitcast.18) | data formatting | bytes 409600

commit v5 on v4

--- a/solution.py
+++ b/solution.py
@@ -289,6 +289,12 @@
     send(rows, rows, rc_s.at[3], rc_r.at[3], sibling)
     lax.fori_loop(PARTICLES_HERE // 4, PARTICLES_HERE // 2, turn_pair, 0)
 
+    wide_norm = jnp.broadcast_to(part_norm, (PARTICLES_HERE, ALL_CLASSES))
+    wide_high = wide_norm.astype(BF16).astype(F32)
+    norm_rows[2] = wide_high
+    norm_rows[3] = wide_norm - wide_high
+    ctf_high, ctf_low = split(ctf_ref[...] * ctf_ref[...])
+
     for n, x_of in enumerate((x, (x + 3) % NX, (x + 1) % NX, x_far)):
         rows = spectra.at[class_rows(x_of, other), :]
         remote(rows, rows, rc_s.at[n], rc_r.at[n], sibling).wait_recv()
@@ -299,7 +305,6 @@
             preferred_element_type=F32,
         ).astype(BF16)
 
-    ctf_high, ctf_low = split(ctf_ref[...] * ctf_ref[...])
     ref_norm = lax.dot_general(
         ctf_high, spectra[:, 0:SIDE], NT, preferred_element_type=F32
     ) + lax.dot_general(ctf_low, spectra[:, 0:SIDE], NT, preferred_element_type=F32)
@@ -307,12 +312,8 @@
         picks, ref_norm, TN, precision=lax.Precision.HIGHEST, preferred_element_type=F32
     )
     picked_high = picked.astype(BF16).astype(F32)
-    wide_norm = jnp.broadcast_to(part_norm, (PARTICLES_HERE, ALL_CLASSES))
-    wide_high = wide_norm.astype(BF16).astype(F32)
     norm_rows[0] = picked_high
     norm_rows[1] = picked - picked_high
-    norm_rows[2] = wide_high
-    norm_rows[3] = wide_norm - wide_high
     sub = lax.broadcasted_iota(jnp.int32, (8, ALL_CLASSES), 0)
 
     def z_group(step):
@@ -597,6 +598,30 @@
             send(
                 via_buf, cut(part, rep_in, half), p2s.at[part, half], p2r.at[part, half], via[half]
             )
+
+    for copy in sent[:-4]:
+        copy.wait_send()
+
+    def drain(step, carry):
+        for way in range(2):
+            piece = near_out.at[step, way]
+            remote(piece, piece, fs.at[step, way], fr.at[step, way], z_pair).wait_send()
+            for half in range(2):
+                remote(
+                    piece, piece, ns.at[step, way, half], nr.at[step, way, half], z_pair
+                ).wait_send()
+            rows = weights.at[0:Y_ROWS, :]
+            remote(rows, rows, wys.at[step, way], wyr.at[step, way], z_pair).wait_send()
+            half = weights.at[0:PAIR_ROWS, :]
+            remote(half, half, wfs.at[step, way], wfr.at[step, way], z_pair).wait_send()
+
+        @pl.when(step < GROUPS - 1)
+        def _():
+            remote(z_out.at[step], z_in.at[step], zs.at[step], zr.at[step], z_pair).wait_send()
+
+        return carry
+
+    lax.fori_loop(0, GROUPS, drain, 0)
 
     density = None
     for part in parts:
@@ -628,29 +653,8 @@
                     padded[pl.ds(start, BLOCK, stride=16), :] = piece if p == 0 else -piece
     out_ref[...] = padded[0 : CLASSES_HERE * 16, :]
 
-    for copy in sent:
+    for copy in sent[-4:]:
         copy.wait_send()
-
-    def drain(step, carry):
-        for way in range(2):
-            piece = near_out.at[step, way]
-            remote(piece, piece, fs.at[step, way], fr.at[step, way], z_pair).wait_send()
-            for half in range(2):
-                remote(
-                    piece, piece, ns.at[step, way, half], nr.at[step, way, half], z_pair
-                ).wait_send()
-            rows = weights.at[0:Y_ROWS, :]
-            remote(rows, rows, wys.at[step, way], wyr.at[step, way], z_pair).wait_send()
-            half = weights.at[0:PAIR_ROWS, :]
-            remote(half, half, wfs.at[step, way], wfr.at[step, way], z_pair).wait_send()
-
-        @pl.when(step < GROUPS - 1)
-        def _():
-            remote(z_out.at[step], z_in.at[step], zs.at[step], zr.at[step], z_pair).wait_send()
-
-        return carry
-
-    lax.fori_loop(0, GROUPS, drain, 0)
 
 
 def to_rows(values):

time: 102 us -> 102 us (level)
  the two profiles are of different devices: /device:TPU:58 before, /device:TPU:47 now
where the time goes in v5:
time: 102 us
  Pallas kernels  100 us (98%)
  local copies, waits for them, and re-layouts  1.62 us (2%)
    pallas_call x1, Pallas kernels, per_device(): pl.pallas_call(body, out_shape=jax.ShapeDtypeStruct((CLASSES_HERE * 16, 1...  100 us

profile of v5, /device:TPU:47, one launch (start us, length us, event | category | flops | bytes accessed | tf_op | source)
XLA Modules:
  0.0 101.7 jit_solution(5878911547492117653)
XLA Ops:
  0.0 100.1 %shard_map.73 = f32[400,128]{1,0:T(8,128)} custom-call(f32[1024,128]{1,0:T(8,128)} %bitcast.19, f32[400,128]{1,0:T(8,128)} %bitcast.20, f32[512,512]{1,0:T(8,128)} %constant.4.clone.dft_hbm, f32[256,256]{1,0:T(8,128)} %constant.5.clone.walsh_hbm, f32[4,16]{1,0:T(4,128)} %bitcast.21, s32[1,64]{1,0:T(1,128)} %bitcast.22, s32[1,36]{1,0:T(1,128)} %bitcast.23), custom_call_target="tpu_custom_call" | custom-call | tf_op jit(solution)/shard_map/pallas_call | solution.py:676
  100.1 1.6 %copy.12 = f32[25,4,2,256]{3,2,1,0:T(2,128)} copy(f32[25,4,2,256]{3,2,1,0:T(2,128)} %bitcast.18) | data formatting | bytes 409600

commit v6 on v5

--- a/solution.py
+++ b/solution.py
@@ -476,14 +476,17 @@
             half = weights.at[y_half_of(group, y_of, way), :]
             start_copy(half, half, wfs.at[step, way], wfr.at[step, way], y_peer(steps[way]))
 
-    def add_group(step):
+    def await_group(step):
         group = w_group(step)
         for way in range(2):
             half = weights.at[y_half_of(group, (y + 2) % NY, way), :]
             remote(
                 half, half, wfs.at[step, way], wfr.at[step, way], y_peer(steps[way])
             ).wait_recv()
-        rows = pl.ds(pl.multiple_of(group * GROUP_ROWS, GROUP_ROWS), GROUP_ROWS)
+        return pl.ds(pl.multiple_of(group * GROUP_ROWS, GROUP_ROWS), GROUP_ROWS)
+
+    def add_group(step):
+        rows = await_group(step)
         picked_weights = weights[rows, :].T
         sums[:, 0:SIDE] += lax.dot_general(
             picked_weights, turned[rows, 0:SIDE], NN, preferred_element_type=F32
@@ -500,7 +503,9 @@
         pl.when(step > 1)(lambda: add_group(step - 2))
         return carry
 
-    lax.fori_loop(0, GROUPS + 2, weight_step, 0)
+    lax.fori_loop(0, GROUPS + 1, weight_step, 0)
+    last_rows = await_group(GROUPS - 1)
+    last_weights = weights[last_rows, :].T
 
     HALF = BLOCK // 2
     parts = (0, 1)
@@ -523,6 +528,12 @@
 
     for part in parts:
         out_buf, in_buf = cut(part, core_out), cut(part, core_in)
+        for n in range(2):
+            first = SIDE + (part * 2 + n) * 512
+            lanes = slice(first if first > SIDE else 0, first + 512)
+            sums[:, lanes] += lax.dot_general(
+                last_weights, turned[last_rows, lanes], NN, preferred_element_type=F32
+            )
         for d in range(NX):
             out_buf[d * BLOCK : (d + 1) * BLOCK, :] = rounded(
                 part, sums[class_rows(d, other), part_lanes[part]]

time: 102 us -> 102 us (level)
  the two profiles are of different devices: /device:TPU:47 before, /device:TPU:42 now
where the time goes in v6:
time: 102 us
  Pallas kernels  100 us (98%)
  local copies, waits for them, and re-layouts  1.62 us (2%)
    pallas_call x1, Pallas kernels, per_device(): pl.pallas_call(body, out_shape=jax.ShapeDtypeStruct((CLASSES_HERE * 16, 1...  100 us

profile of v6, /device:TPU:42, one launch (start us, length us, event | category | flops | bytes accessed | tf_op | source)
XLA Modules:
  0.0 101.6 jit_solution(9175927351647904269)
XLA Ops:
  0.0 100.0 %shard_map.73 = f32[400,128]{1,0:T(8,128)} custom-call(f32[1024,128]{1,0:T(8,128)} %bitcast.19, f32[400,128]{1,0:T(8,128)} %bitcast.20, f32[512,512]{1,0:T(8,128)} %constant.4.clone.dft_hbm, f32[256,256]{1,0:T(8,128)} %constant.5.clone.walsh_hbm, f32[4,16]{1,0:T(4,128)} %bitcast.21, s32[1,64]{1,0:T(1,128)} %bitcast.22, s32[1,36]{1,0:T(1,128)} %bitcast.23), custom_call_target="tpu_custom_call" | custom-call | tf_op jit(solution)/shard_map/pallas_call | solution.py:687
  100.0 1.6 %copy.12 = f32[25,4,2,256]{3,2,1,0:T(2,128)} copy(f32[25,4,2,256]{3,2,1,0:T(2,128)} %bitcast.18) | data formatting | bytes 409600

commit v7 on v6

--- a/solution.py
+++ b/solution.py
@@ -353,12 +353,6 @@
                 partial.at[y_half_of(group, (y + 2) % NY, way), :],
                 far_in.at[step, way], fs.at[step, way], fr.at[step, way], y_peer(steps[way]),
             )
-        for way in range(2):
-            start_copy(
-                partial.at[y_half_of(group, (y + steps[way]) % NY, 1 - way), :],
-                near_in.at[step, way, 1 - way],
-                ns.at[step, way, 1 - way], nr.at[step, way, 1 - way], y_peer(steps[way]),
-            )
 
     odd_row = sub % 2 == 1
 
@@ -381,24 +375,27 @@
             remote(
                 own, far_in.at[step, way], fs.at[step, way], fr.at[step, way], y_peer(steps[way])
             ).wait_recv()
-            near_out[step, way] = product_rounded(
+            near_out[step, way, way] = product_rounded(
                 own[...].astype(F32) + far_in[step, way].astype(F32)
             )
+            near_out[step, way, 1 - way] = partial[
+                y_half_of(group, (y + steps[way]) % NY, 1 - way), :
+            ]
             start_copy(
-                near_out.at[step, way], near_in.at[step, way, way],
-                ns.at[step, way, way], nr.at[step, way, way], y_peer(steps[way]),
+                near_out.at[step, way], near_in.at[step, way],
+                ns.at[step, way], nr.at[step, way], y_peer(steps[way]),
             )
 
     def reduce_y(step):
         group = z_group(step)
+        for way in range(2):
+            remote(
+                near_out.at[step, way], near_in.at[step, way],
+                ns.at[step, way], nr.at[step, way], y_peer(steps[way]),
+            ).wait_recv()
         for half in range(2):
-            own = partial.at[y_half_of(group, y, half), :]
-            total = own[...].astype(F32)
+            total = partial[y_half_of(group, y, half), :].astype(F32)
             for way in range(2):
-                remote(
-                    own, near_in.at[step, way, half],
-                    ns.at[step, way, half], nr.at[step, way, half], y_peer(steps[way]),
-                ).wait_recv()
                 total += near_in[step, way, half].astype(F32)
             z_out[step, half * PAIR_ROWS : (half + 1) * PAIR_ROWS, :] = product_rounded(total)
 
@@ -615,12 +612,10 @@
 
     def drain(step, carry):
         for way in range(2):
+            piece = far_in.at[step, way]
+            remote(piece, piece, fs.at[step, way], fr.at[step, way], z_pair).wait_send()
             piece = near_out.at[step, way]
-            remote(piece, piece, fs.at[step, way], fr.at[step, way], z_pair).wait_send()
-            for half in range(2):
-                remote(
-                    piece, piece, ns.at[step, way, half], nr.at[step, way, half], z_pair
-                ).wait_send()
+            remote(piece, piece, ns.at[step, way], nr.at[step, way], z_pair).wait_send()
             rows = weights.at[0:Y_ROWS, :]
             remote(rows, rows, wys.at[step, way], wyr.at[step, way], z_pair).wait_send()
             half = weights.at[0:PAIR_ROWS, :]
@@ -715,7 +710,7 @@
             pltpu.VMEM((ALL_ROWS, ALL_CLASSES), BF16),
             pltpu.VMEM((GROUPS, 2, PAIR_ROWS, ALL_CLASSES), BF16),
             pltpu.VMEM((GROUPS, 2, 2, PAIR_ROWS, ALL_CLASSES), BF16),
-            pltpu.VMEM((GROUPS, 2, PAIR_ROWS, ALL_CLASSES), BF16),
+            pltpu.VMEM((GROUPS, 2, 2, PAIR_ROWS, ALL_CLASSES), BF16),
             pltpu.VMEM((GROUPS, Y_ROWS, ALL_CLASSES), BF16),
             pltpu.VMEM((GROUPS - 1, Y_ROWS, ALL_CLASSES), BF16),
             pltpu.VMEM((Y_ROWS, ALL_CLASSES), BF16),
@@ -735,7 +730,7 @@
             dma((2,)), dma((2,)), dma((2,)), dma((2,)),
             dma((NX,)), dma((NX,)),
             dma((GROUPS, 2)), dma((GROUPS, 2)),
-            dma((GROUPS, 2, 2)), dma((GROUPS, 2, 2)),
+            dma((GROUPS, 2)), dma((GROUPS, 2)),
             dma((GROUPS - 1,)), dma((GROUPS - 1,)),
             dma(()), dma(()),
             dma((GROUPS,)), dma((GROUPS,)),

time: 102 us -> 101 us (level)
  the two profiles are of different devices: /device:TPU:42 before, /device:TPU:1 now
where the time goes in v7:
time: 101 us; the launch traced here: 100 us
  Pallas kernels  98.8 us (98%)
  local copies, waits for them, and re-layouts  1.62 us (2%)
    pallas_call x1, Pallas kernels, per_device(): pl.pallas_call(body, out_shape=jax.ShapeDtypeStruct((CLASSES_HERE * 16, 1...  98.8 us

profile of v7, /device:TPU:1, one launch (start us, length us, event | category | flops | bytes accessed | tf_op | source)
XLA Modules:
  0.0 100.5 jit_solution(12858468895098790845)
XLA Ops:
  0.0 98.8 %shard_map.73 = f32[400,128]{1,0:T(8,128)} custom-call(f32[1024,128]{1,0:T(8,128)} %bitcast.19, f32[400,128]{1,0:T(8,128)} %bitcast.20, f32[512,512]{1,0:T(8,128)} %constant.4.clone.dft_hbm, f32[256,256]{1,0:T(8,128)} %constant.5.clone.walsh_hbm, f32[4,16]{1,0:T(4,128)} %bitcast.21, s32[1,64]{1,0:T(1,128)} %bitcast.22, s32[1,36]{1,0:T(1,128)} %bitcast.23), custom_call_target="tpu_custom_call" | custom-call | tf_op jit(solution)/shard_map/pallas_call | solution.py:682
  98.8 1.6 %copy.12 = f32[25,4,2,256]{3,2,1,0:T(2,128)} copy(f32[25,4,2,256]{3,2,1,0:T(2,128)} %bitcast.18) | data formatting | bytes 409600
